TPU v7x, 32 devices: a whole 2x2x4 slice. The times are simulated.
32 devices in a mesh: gx: 8 (over z, x), gy: 4 (over y, core).
Axes of the slice: x: 2, y: 2, z: 4, core: 2. Of those that a mesh axis runs over, the one named last changes fastest.
Arguments:
- tokens: bfloat16 [512, 4096], P('gy', 'gx'), may hold values from -6 to 6
- attn_gain: bfloat16 [4096], replicated, may hold values from 0.099609375 to 1.8984375
- qkv_weight: bfloat16 [4096, 6144], P('gy', 'gx'), may hold values from -0.1875 to 0.1875
- out_weight: bfloat16 [4096, 4096], P('gx', 'gy'), may hold values from -0.09375 to 0.09375
- mlp_gain: bfloat16 [4096], replicated, may hold values from 0.099609375 to 1.8984375
- up_weight: bfloat16 [4096, 12288], P('gy', 'gx'), may hold values from -0.09375 to 0.09375
- down_weight: bfloat16 [12288, 4096], P('gx', 'gy'), may hold values from -0.0546875 to 0.0546875
- final_gain: bfloat16 [4096], replicated, may hold values from 0.099609375 to 1.8984375
- head_weight: bfloat16 [4096, 131072], P(None, ('gx', 'gy')), may hold values from -0.25 to 0.25
- kv_cache: bfloat16 [32, 4096, 256], P(('gy', 'gx')), may hold values from -40 to 40
- cache_lengths: int32 [4], replicated, may hold values from 1 to 3968, as said below
- slot_request: int32 [4], replicated, may hold values from 0 to 3, each once
Outputs:
- hidden_out: bfloat16 [512, 4096], P('gy', 'gx')
- new_cache: bfloat16 [32, 4096, 256], P(('gy', 'gx'))
- last_norms: float32 [4], replicated
- max_logits: float32 [4], replicated
- head_input: bfloat16 [4, 4096], replicated
Inputs may be any that keep to these rules, and one draw needn't show every extreme that they name: `cache_lengths`: the longest request has exactly 3968 cached positions.
All inputs are finite; a program needn't handle non-finite values.
Results may differ from a plain program's by a relative error of at most 0.02.
The roundings to bfloat16 on the way count: a program that leaves them out, or rounds other values in their place, can miss the bound.
Values may be sent and summed in bfloat16 or wider, within the bound.
No kernel may reach another device: no remote copies, remote signals or barrier semaphores. Data moves between devices by JAX's collectives and lax.ppermute only.
A program may use at most 128 MiB of HBM per device.

v0:
```python
import math

import jax
import jax.numpy as jnp
from jax import lax
from jax.sharding import PartitionSpec as P

HEADS = 32
KVH = 8
HD = 128


epsilon = 1e-05
negative = -1e30


def from_partner(block, axis, distance):
    count = lax.axis_size(axis)
    route = []
    for low in range(count):
        high = low | 1 << distance
        if high != low and high < count:
            route += [(low, high), (high, low)]
    return lax.ppermute(block, axis, route)


def rms_factor(row_block):
    return lax.rsqrt(jnp.mean(row_block * row_block, axis=-1, keepdims=True) + epsilon)


def gather_features(shard_rows):
    return lax.all_gather(shard_rows, "gx", axis=1, tiled=True)


def rows_product(left_rows, weight_shard):
    return jnp.dot(
        left_rows,
        lax.all_gather(weight_shard, "gy", axis=0, tiled=True),
        preferred_element_type=jnp.float32,
    )


def columns_product(left_rows, weight_shard):
    return jnp.dot(
        left_rows,
        lax.all_gather(weight_shard, "gy", axis=1, tiled=True),
        preferred_element_type=jnp.float32,
    )


def pair_swap(values):
    return from_partner(values, "gx", KVH.bit_length() - 1)


def scatter_partials(partial_terms):
    return lax.psum_scatter(
        partial_terms.astype(jnp.bfloat16), "gx", scatter_dimension=1, tiled=True
    ).astype(jnp.float32)


def merge_block(carried, scores, value_rows):
    row_max, running, numerator = carried
    new_max = jnp.maximum(row_max, jnp.max(scores, axis=1, keepdims=True))
    factor = jnp.exp(row_max - new_max)
    weights = jnp.exp(scores - new_max)
    running = running * factor + jnp.sum(weights, axis=1, keepdims=True)
    numerator = numerator * factor + jnp.dot(
        weights.astype(jnp.bfloat16), value_rows, preferred_element_type=jnp.float32
    )
    return (new_max, running, numerator)


def attend_cache(group_cols, cache_rows, length, new_rows):
    per_group = HEADS // KVH
    scaling = 1.0 / math.sqrt(HD)
    query_rows = per_group * new_rows
    queries = (
        group_cols[:, : per_group * HD]
        .reshape(new_rows, per_group, HD)
        .transpose(1, 0, 2)
        .reshape(query_rows, HD)
    )
    key_new = group_cols[:, per_group * HD : (per_group + 1) * HD]
    value_new = group_cols[:, (per_group + 1) * HD :]
    block_len = min(512, cache_rows.shape[0])

    def visit_block(step_index, carried):
        offset = step_index * block_len
        block_rows = lax.dynamic_slice_in_dim(cache_rows, offset, block_len, 0)
        scores = (
            jnp.dot(queries, block_rows[:, :HD].T, preferred_element_type=jnp.float32) * scaling
        )
        positions = offset + jnp.arange(block_len)
        scores = jnp.where(positions[None, :] < length, scores, negative)
        return merge_block(carried, scores, block_rows[:, HD:])

    initial = (
        jnp.full((query_rows, 1), negative, jnp.float32),
        jnp.zeros((query_rows, 1), jnp.float32),
        jnp.zeros((query_rows, HD), jnp.float32),
    )
    block_count = (length + block_len - 1) // block_len
    carried = lax.fori_loop(0, block_count, visit_block, initial)
    new_scores = jnp.dot(queries, key_new.T, preferred_element_type=jnp.float32) * scaling
    causal = jnp.arange(new_rows)[None, :] <= (jnp.arange(query_rows) % new_rows)[:, None]
    new_scores = jnp.where(causal, new_scores, negative)
    row_max, running, numerator = merge_block(carried, new_scores, value_new)
    attended = (numerator / running).astype(jnp.bfloat16)
    attended = (
        attended.reshape(per_group, new_rows, HD)
        .transpose(1, 0, 2)
        .reshape(new_rows, per_group * HD)
    )
    fresh = jnp.concatenate([key_new, value_new], axis=1)
    appended = lax.dynamic_update_slice(cache_rows, fresh, (length, jnp.zeros((), jnp.int32)))
    return (attended, appended)


def local(
    tokens,
    attn_gain,
    qkv_weight,
    out_weight,
    mlp_gain,
    up_weight,
    down_weight,
    final_gain,
    head_weight,
    kv_cache,
    cache_lengths,
    slot_request,
):
    gx_count = lax.axis_size("gx")
    gy_count = lax.axis_size("gy")
    copies = gx_count // KVH
    gx_place = lax.axis_index("gx")
    copy_index = gx_place // KVH
    slot_index = lax.axis_index("gy") * copies + copy_index
    new_rows = tokens.shape[0] // copies
    feature_cols = tokens.shape[1]
    gathered_tokens = gather_features(tokens)
    tokens_f32 = gathered_tokens.astype(jnp.float32)
    normed = (tokens_f32 * rms_factor(tokens_f32) * attn_gain.astype(jnp.float32)).astype(
        jnp.bfloat16
    )
    projected = rows_product(normed, qkv_weight).astype(jnp.bfloat16)
    if copies == 2:
        own_half = lax.dynamic_slice_in_dim(projected, copy_index * new_rows, new_rows, 0)
        sent_rows = lax.dynamic_slice_in_dim(projected, (1 - copy_index) * new_rows, new_rows, 0)
        received = pair_swap(sent_rows)
        group_cols = jnp.where(
            copy_index == 0,
            jnp.concatenate([own_half, received], axis=1),
            jnp.concatenate([received, own_half], axis=1),
        )
    else:
        group_cols = projected
    length = cache_lengths[slot_request[slot_index]]
    attended, appended = attend_cache(group_cols, kv_cache[0], length, new_rows)
    new_cache = appended[None]
    if copies == 2:
        half_width = attended.shape[1] // 2
        kept_half = lax.dynamic_slice_in_dim(attended, copy_index * half_width, half_width, 1)
        handed = lax.dynamic_slice_in_dim(attended, (1 - copy_index) * half_width, half_width, 1)
        returned = pair_swap(handed)
        attention_rows = jnp.where(
            copy_index == 0,
            jnp.concatenate([kept_half, returned], axis=0),
            jnp.concatenate([returned, kept_half], axis=0),
        )
    else:
        attention_rows = attended
    attention_terms = columns_product(attention_rows, out_weight)
    middle = (tokens.astype(jnp.float32) + scatter_partials(attention_terms)).astype(jnp.bfloat16)
    middle_full = gather_features(middle)
    middle_f32 = middle_full.astype(jnp.float32)
    mlp_input = (middle_f32 * rms_factor(middle_f32) * mlp_gain.astype(jnp.float32)).astype(
        jnp.bfloat16
    )
    up_values = rows_product(mlp_input, up_weight)
    rectified = jnp.maximum(up_values, 0.0)
    activation = (rectified * rectified).astype(jnp.bfloat16)
    down_terms = columns_product(activation, down_weight)
    hidden_out = (middle.astype(jnp.float32) + scatter_partials(down_terms)).astype(jnp.bfloat16)
    final_rows = hidden_out.reshape(copies, new_rows, feature_cols)[:, new_rows - 1, :]
    every_last = lax.all_gather(final_rows, ("gx", "gy"), axis=0, tiled=True)
    slot_rows = every_last.reshape(gx_count, gy_count, copies, feature_cols).transpose(1, 2, 0, 3)
    slot_rows = slot_rows.reshape(gy_count * copies, gx_count * feature_cols).astype(jnp.float32)
    mean_square = jnp.mean(slot_rows * slot_rows, axis=1)
    last_norms = jnp.sqrt(mean_square)
    head_input = (
        slot_rows * lax.rsqrt(mean_square + epsilon)[:, None] * final_gain.astype(jnp.float32)
    ).astype(jnp.bfloat16)
    logits = jnp.dot(head_input, head_weight, preferred_element_type=jnp.float32)
    max_logits = lax.pmax(jnp.max(logits, axis=1), ("gx", "gy"))
    return (hidden_out, new_cache, last_norms, max_logits, head_input)


def solution(mesh):
    in_specs = (
        P("gy", "gx"),
        P(),
        P("gy", "gx"),
        P("gx", "gy"),
        P(),
        P("gy", "gx"),
        P("gx", "gy"),
        P(),
        P(None, ("gx", "gy")),
        P(("gy", "gx"), None, None),
        P(),
        P(),
    )
    out_specs = (P("gy", "gx"), P(("gy", "gx"), None, None), P(), P(), P())
    return jax.shard_map(local, mesh=mesh, in_specs=in_specs, out_specs=out_specs, check_vma=False)
```

profile of v0, /device:TPU:0, one launch (start us, length us, event | category | flops | bytes accessed | tf_op | source)
XLA Modules:
  0.0 587.1 jit_solution(1318768004866995659)
XLA Ops:
  7.9 0.7 all-gather.10.cloned.1.call-update
  13.3 39.0 %all-gather.8.cloned.1.call-done = bf16[128,4096]{1,0:T(8,128)(2,1)} async-done(((bf16[128,512]{1,0:T(8,128)(2,1)}), bf16[128,4096]{1,0:T(8,128)(2,1)}) %all-gather.8.cloned.1.call-update) | async-done | bytes 1048592 | tf_op jit(solution)/shard_map/all_gather | solution.py:32
  52.3 1.5 fusion.10
  53.8 45.3 %all-gather.10.cloned.1.call-done = bf16[4096,768]{1,0:T(8,128)(2,1)} async-done(((bf16[1024,768]{1,0:T(8,128)(2,1)}), bf16[4096,768]{1,0:T(8,128)(2,1)}) %all-gather.10.cloned.1.call-update) | async-done | bytes 6291472 | tf_op jit(solution)/shard_map/all_gather | solution.py:38
  99.2 4.2 convolution_convert_fusion.2
  103.4 1.5 fusion.39
  105.0 3.3 while.14
  109.0 1.1 fusion.28
  110.1 1.2 fusion.18
  111.5 23.8 %all-gather.12.cloned.1.call-done = bf16[512,4096]{1,0:T(8,128)(2,1)} async-done(((bf16[512,1024]{1,0:T(8,128)(2,1)}), bf16[512,4096]{1,0:T(8,128)(2,1)}) %all-gather.12.cloned.1.call-update) | async-done | bytes 4194320 | tf_op jit(solution)/shard_map/all_gather | solution.py:46
  135.3 3.9 convolution_convert_fusion.1
  139.3 64.0 %reduce-scatter.3.cloned.1.call-done = bf16[128,512]{1,0:T(8,128)(2,1)} async-done(((bf16[128,4096]{1,0:T(8,128)(2,1)}), bf16[128,512]{1,0:T(8,128)(2,1)}) %reduce-scatter.3.cloned.1.call-update) | async-done | bytes 131088 | tf_op jit(solution)/shard_map/reduce_scatter | solution.py:56
  203.3 1.6 add_convert_fusion.1
  206.3 38.2 %all-gather.14.cloned.1.call-done = bf16[128,4096]{1,0:T(8,128)(2,1)} async-done(((bf16[128,512]{1,0:T(8,128)(2,1)}), bf16[128,4096]{1,0:T(8,128)(2,1)}) %all-gather.14.cloned.1.call-update) | async-done | bytes 1048592 | tf_op jit(solution)/shard_map/all_gather | solution.py:32
  244.5 1.5 fusion.13
  246.0 81.0 %all-gather.16.cloned.1.call-done = bf16[4096,1536]{1,0:T(8,128)(2,1)} async-done(((bf16[1024,1536]{1,0:T(8,128)(2,1)}), bf16[4096,1536]{1,0:T(8,128)(2,1)}) %all-gather.16.cloned.1.call-update) | async-done | bytes 12582928 | tf_op jit(solution)/shard_map/all_gather | solution.py:38
  327.0 83.8 %all-gather.18.cloned.1.call-done = bf16[1536,4096]{1,0:T(8,128)(2,1)} async-done(((bf16[1536,1024]{1,0:T(8,128)(2,1)}), bf16[1536,4096]{1,0:T(8,128)(2,1)}) %all-gather.18.cloned.1.call-update) | async-done | bytes 12582928 | tf_op jit(solution)/shard_map/all_gather | solution.py:46
  410.8 12.9 %convolution_convert_fusion = bf16[128,4096]{1,0:T(8,128)(2,1)} fusion(bf16[1536,4096]{1,0:T(8,128)(2,1)} %all-gather.18.cloned.1.call-done, bf16[4096,1536]{1,0:T(8,128)(2,1)} %all-gather.16.cloned.1.call-done, bf16[128,4096]{1,0:T(8,128)(2,1)} %all-gather.14.cloned.1.call-done, f32[4096]{0:T(1024)S(1)} %convert_element_type.90, f32[128]{0:T(128)S(1)} %add_rsqrt_fusion.1), kind=kOutput, calls=%fused_computation.13 | convolution fusion | flops 3224436736 | bytes 27279872 | tf_op jit(solution)/shard_map/dot_general | solution.py:44
  425.7 0.8 slice_bitcast_fusion
  426.5 61.3 %reduce-scatter.5.cloned.1.call-done = bf16[128,512]{1,0:T(8,128)(2,1)} async-done(((bf16[128,4096]{1,0:T(8,128)(2,1)}), bf16[128,512]{1,0:T(8,128)(2,1)}) %reduce-scatter.5.cloned.1.call-update) | async-done | bytes 131088 | tf_op jit(solution)/shard_map/reduce_scatter | solution.py:56
  487.9 0.9 add_convert_fusion
  488.8 39.7 %all-gather = bf16[32,1,512]{2,1,0:T(2,128)(2,1)S(1)} all-gather(bf16[1,1,512]{2,1,0:T(2,128)(2,1)S(1)} %slice.26), channel_id=2, replica_groups=mesh['gx'=8,'gy'=4] {'gx','gy'}, dimensions={0}, use_global_device_ids=true | all-gather | bytes 33792 | tf_op jit(solution)/shard_map/all_gather | solution.py:186
  529.7 13.0 %convolution_reduce_fusion = f32[4]{0:T(128)S(1)} fusion(bf16[4,4096]{1,0:T(4,128)(2,1)S(1)} %multiply_convert_fusion, bf16[4096,4096]{1,0:T(8,128)(2,1)} %param.22), kind=kOutput, calls=%fused_computation.34 | convolution fusion | flops 134234112 | bytes 33587216 | tf_op jit(solution)/shard_map/dot_general | solution.py:194
  543.3 36.9 %pmax.7 = f32[4]{0:T(128)} all-reduce(f32[4]{0:T(128)S(1)} %convolution_reduce_fusion), channel_id=1, replica_groups=mesh['gx'=8,'gy'=4] {'gx','gy'}, use_global_device_ids=true, to_apply=%region_13.14 | all-reduce | flops 4 | bytes 32 | tf_op jit(solution)/shard_map/pmax | solution.py:195
  (80 shorter events, 10.1 us)
Async XLA Ops:
  7.2 45.1 %all-gather.8.cloned.1.call-start = ((), (), s32[]{:S(2)}) async-start(), calls=%async_computation.2 | async-start | bytes 1179648 | tf_op jit(solution)/shard_map/all_gather | solution.py:32
  7.2 2.2 copy-start.10
  7.2 4.8 copy-start.11
  7.2 6.0 %copy-start.7 = (bf16[4096]{0:T(1024)(128)(2,1)S(1)}, bf16[4096]{0:T(1024)(128)(2,1)}, u32[]{:S(2)}) copy-start(bf16[4096]{0:T(1024)(128)(2,1)} %param.15) | copy-start | bytes 24580
  7.9 91.3 %all-gather.10.cloned.1.call-start = ((), (), s32[]{:S(2)}) async-start(), calls=%async_computation.3 | async-start | bytes 7864320 | tf_op jit(solution)/shard_map/all_gather | solution.py:38
  8.6 126.6 %all-gather.12.cloned.1.call-start = ((), (), s32[]{:S(2)}) async-start(), calls=%async_computation.4 | async-start | bytes 5242880 | tf_op jit(solution)/shard_map/all_gather | solution.py:46
  9.4 193.9 %reduce-scatter.3.cloned.1.call-start = ((), (), s32[]{:S(2)}) async-start(), calls=%async_computation.5 | async-start | bytes 1179648 | tf_op jit(solution)/shard_map/reduce_scatter | solution.py:56
  53.8 51.1 %copy-start.1 = (bf16[1,4096,256]{2,1,0:T(8,128)(2,1)S(1)}, bf16[1,4096,256]{2,1,0:T(8,128)(2,1)}, u32[]{:S(2)}) copy-start(bf16[1,4096,256]{2,1,0:T(8,128)(2,1)} %param.23) | copy-start | bytes 6291460
  103.3 1.6 copy-start.4
  135.3 68.0 %copy-start.3 = (bf16[128,512]{1,0:T(8,128)(2,1)S(1)}, bf16[128,512]{1,0:T(8,128)(2,1)}, u32[]{:S(2)}) copy-start(bf16[128,512]{1,0:T(8,128)(2,1)} %param.14) | copy-start | bytes 393220
  139.2 105.3 %all-gather.14.cloned.1.call-start = ((), (), s32[]{:S(2)}) async-start(), calls=%async_computation.6 | async-start | bytes 1179648 | tf_op jit(solution)/shard_map/all_gather | solution.py:32
  204.9 122.1 %all-gather.16.cloned.1.call-start = ((), (), s32[]{:S(2)}) async-start(), calls=%async_computation.7 | async-start | bytes 15728640 | tf_op jit(solution)/shard_map/all_gather | solution.py:38
  205.5 0.8 copy-start.8
  205.5 205.3 %all-gather.18.cloned.1.call-start = ((), (), s32[]{:S(2)}) async-start(), calls=%async_computation.8 | async-start | bytes 15728640 | tf_op jit(solution)/shard_map/all_gather | solution.py:46
  206.2 281.6 %reduce-scatter.5.cloned.1.call-start = ((), (), s32[]{:S(2)}) async-start(), calls=%async_computation.9 | async-start | bytes 1179648 | tf_op jit(solution)/shard_map/reduce_scatter | solution.py:56
  246.0 179.0 %copy-start.9 = (bf16[4096]{0:T(1024)(128)(2,1)S(1)}, bf16[4096]{0:T(1024)(128)(2,1)}, u32[]{:S(2)}) copy-start(bf16[4096]{0:T(1024)(128)(2,1)} %param.21) | copy-start | bytes 24580
  246.0 241.8 %copy-start.2 = (bf16[128,512]{1,0:T(8,128)(2,1)S(1)}, bf16[128,512]{1,0:T(8,128)(2,1)}, u32[]{:S(2)}) copy-start(bf16[128,512]{1,0:T(8,128)(2,1)} %add_convert_fusion.1) | copy-start | bytes 393220
  488.8 53.9 %copy-start.6 = (bf16[128,512]{1,0:T(8,128)(2,1)}, bf16[128,512]{1,0:T(8,128)(2,1)S(1)}, u32[]{:S(2)}) copy-start(bf16[128,512]{1,0:T(8,128)(2,1)S(1)} %add_convert_fusion) | copy-start | bytes 393220
  529.7 13.0 %copy-start.5 = (bf16[4,4096]{1,0:T(4,128)(2,1)}, bf16[4,4096]{1,0:T(4,128)(2,1)S(1)}, u32[]{:S(2)}) copy-start(bf16[4,4096]{1,0:T(4,128)(2,1)S(1)} %multiply_convert_fusion) | copy-start | bytes 98308
  543.3 36.9 %copy-start = (bf16[1,4096,256]{2,1,0:T(8,128)(2,1)}, bf16[1,4096,256]{2,1,0:T(8,128)(2,1)S(1)}, u32[]{:S(2)}) copy-start(bf16[1,4096,256]{2,1,0:T(8,128)(2,1)S(1)} %dynamic_update_slice.4) | copy-start | bytes 6291460
Sparse Core Ops, SparseCore 0:
  10.0 42.2 all-gather.7
  53.9 45.2 all-gather.9
  100.7 34.4 all-gather.11
  139.4 63.8 reduce-scatter.2
  205.9 38.5 all-gather.13
  246.0 80.9 all-gather.15
  328.6 82.0 all-gather.17
  423.8 63.9 reduce-scatter.4
where the time goes:
time: 588 us; the launch traced here: 587 us
  waiting for transfers between devices  440 us (75%)
  blocking collectives  76.6 us (13%)
  matrix products  38.1 us (6%)
  between operations  19 us (3%)
  other arithmetic  10.2 us (2%)
    all_gather x2, waiting for transfers between devices, rows_product(): lax.all_gather(weight_shard, 'gy', axis=0, tiled=True)  126 us
    reduce_scatter x2, waiting for transfers between devices, scatter_partials(): lax.psum_scatter(partial_terms.astype(jnp.bfloat16), 'gx', scatter_dimens...  125 us
    all_gather x2, waiting for transfers between devices, columns_product(): lax.all_gather(weight_shard, 'gy', axis=1, tiled=True)  108 us
    all_gather x2, waiting for transfers between devices, gather_features(): return lax.all_gather(shard_rows, 'gx', axis=1, tiled=True)  77.2 us
    all_gather x1, blocking collectives, local(): every_last = lax.all_gather(final_rows, ('gx', 'gy'), axis=0, tiled=True)  39.7 us
    pmax x1, blocking collectives, local(): max_logits = lax.pmax(jnp.max(logits, axis=1), ('gx', 'gy'))  36.9 us
    dot_general x2, matrix products, columns_product(): jnp.dot(left_rows, lax.all_gather(weight_shard, 'gy', axis=1, tiled=True)...  16.8 us
    dot_general x1, matrix products, local(): jnp.dot(head_input, head_weight, preferred_element_type=jnp.float32)  13 us
  transfers between devices with their start and end apart: 8, of which 8 were waited for; matrix products, arithmetic and copies ran while one was open for 3% of the time, Pallas kernels for 0%

commit v1 on v0

--- a/solution.py
+++ b/solution.py
@@ -3,6 +3,8 @@
 import jax
 import jax.numpy as jnp
 from jax import lax
+from jax.experimental import pallas as pl
+from jax.experimental.pallas import tpu as pltpu
 from jax.sharding import PartitionSpec as P
 
 HEADS = 32
@@ -196,7 +198,594 @@
     return (hidden_out, new_cache, last_norms, max_logits, head_input)
 
 
+def xor_permute(values, axis, distance):
+    count = lax.axis_size(axis)
+    return lax.ppermute(values, axis, [(place, place ^ distance) for place in range(count)])
+
+
+def transpose_places(block):
+    gx_count, gy_count = lax.axis_size("gx"), lax.axis_size("gy")
+    halves = gx_count // gy_count
+    route = []
+    for gx_at in range(gx_count):
+        for gy_at in range(gy_count):
+            target = (gy_at * halves + gx_at % halves) * gy_count + gx_at // halves
+            route.append((gx_at * gy_count + gy_at, target))
+    return lax.ppermute(block, ("gx", "gy"), route)
+
+
+def exchange(blocks, axes):
+    return lax.all_to_all(blocks, axes, split_axis=0, concat_axis=0, tiled=True)
+
+
+def across(block, places):
+    return xor_permute(block, "gx", places)
+
+
+PAIRS = tuple((far, near) for far in range(4) for near in range(2))
+
+
+def gather_blocks(block):
+    found = {(0, 0): block, (0, 1): across(block, 1)}
+    for far in (1, 2, 3):
+        found[far, 0] = across(block, 2 * far)
+    for far in (1, 2, 3):
+        found[far, 1] = across(found[far, 0], 1)
+    return [found[at] for at in PAIRS]
+
+
+def scatter_blocks(blocks, tie=None):
+    held = dict(zip(PAIRS, blocks))
+
+    def wide(values):
+        return values.astype(jnp.float32)
+
+    pairs = [wide(held[far, 0]) + wide(across(held[far, 1], 1)) for far in (2, 3)]
+    pairs = [pair.astype(jnp.bfloat16) for pair in pairs]
+    if tie is not None:
+        *pairs, _ = lax.optimization_barrier((*pairs, tie))
+    summed = [across(pair, 2 * far) for far, pair in zip((2, 3), pairs)]
+    near = wide(across(held[1, 0], 2)) + wide(across(held[1, 1], 3))
+    near = near + wide(held[0, 0]) + wide(across(held[0, 1], 1))
+    return near + wide(summed[0]) + wide(summed[1])
+
+
+def rows_dot(left, weight):
+    return lax.dot_general(
+        left, weight, (((left.ndim - 1,), (0,)), ((), ())), preferred_element_type=jnp.float32
+    )
+
+
+def attend_kernel(
+    place_ref,
+    lengths_ref,
+    requests_ref,
+    group_ref,
+    cache_ref,
+    out_ref,
+    appended_ref,
+    rows_ref,
+    window_ref,
+    numer_ref,
+    max_ref,
+    sum_ref,
+    load_sems,
+    copy_sem,
+    window_sem,
+):
+    per_group = HEADS // KVH
+    new_rows = group_ref.shape[0]
+    query_rows = per_group * new_rows
+    block_len = rows_ref.shape[1]
+    block_count = rows_ref.shape[0]
+    scaling = math.log2(math.e) / math.sqrt(HD)
+    length = lengths_ref[requests_ref[place_ref[0]]]
+
+    def load(step):
+        source = cache_ref.at[pl.ds(pl.multiple_of(step * block_len, block_len), block_len)]
+        return pltpu.make_async_copy(source, rows_ref.at[step], load_sems.at[step])
+
+    for step in range(block_count):
+        load(step).start()
+    whole_copy = pltpu.make_async_copy(cache_ref, appended_ref, copy_sem)
+    whole_copy.start()
+    queries = jnp.concatenate(
+        [group_ref[:, head * HD : (head + 1) * HD] for head in range(per_group)], axis=0
+    )
+    key_new = group_ref[:, per_group * HD : (per_group + 1) * HD]
+    value_new = group_ref[:, (per_group + 1) * HD :]
+
+    def scores_of(keys):
+        products = lax.dot_general(
+            keys, queries, (((1,), (1,)), ((), ())), preferred_element_type=jnp.float32
+        )
+        return products * scaling
+
+    def weigh(weights, values):
+        return lax.dot_general(
+            values,
+            weights.astype(jnp.bfloat16),
+            (((0,), (0,)), ((), ())),
+            preferred_element_type=jnp.float32,
+        )
+
+    def merge(scores, values):
+        old_max = max_ref[...]
+        new_max = jnp.maximum(old_max, jnp.max(scores, axis=0, keepdims=True))
+        factor = jnp.exp2(old_max - new_max)
+        weights = jnp.exp2(scores - new_max)
+        max_ref[...] = new_max
+        sum_ref[...] = sum_ref[...] * factor + jnp.sum(weights, axis=0, keepdims=True)
+        numer_ref[...] = numer_ref[...] * factor + weigh(weights, values)
+
+    key_at = lax.broadcasted_iota(jnp.int32, (new_rows, query_rows), 0)
+    token_at = lax.broadcasted_iota(jnp.int32, (new_rows, query_rows), 1) % new_rows
+    scores = jnp.where(key_at <= token_at, scores_of(key_new), negative)
+    first_max = jnp.max(scores, axis=0, keepdims=True)
+    weights = jnp.exp2(scores - first_max)
+    max_ref[...] = first_max
+    sum_ref[...] = jnp.sum(weights, axis=0, keepdims=True)
+    numer_ref[...] = weigh(weights, value_new)
+
+    def visit(step, carried):
+        load(step).wait()
+        offset = step * block_len
+
+        @pl.when(offset + block_len <= length)
+        def _():
+            merge(scores_of(rows_ref[step, :, :HD]), rows_ref[step, :, HD:])
+
+        @pl.when(jnp.logical_and(offset < length, offset + block_len > length))
+        def _():
+            position = offset + lax.broadcasted_iota(jnp.int32, (block_len, query_rows), 0)
+            scores = jnp.where(position < length, scores_of(rows_ref[step, :, :HD]), negative)
+            merge(scores, rows_ref[step, :, HD:])
+
+        return carried
+
+    lax.fori_loop(0, block_count, visit, 0)
+
+    whole_copy.wait()
+    window_rows = window_ref.shape[0]
+    tile = window_rows - new_rows
+    start = jnp.minimum(length // tile * tile, cache_ref.shape[0] - window_rows)
+    start = pl.multiple_of(start, tile)
+    fetch = pltpu.make_async_copy(cache_ref.at[pl.ds(start, window_rows)], window_ref, window_sem)
+    fetch.start()
+    attended = (numer_ref[...] / sum_ref[...]).T.astype(out_ref.dtype)
+    for head in range(per_group):
+        out_ref[:, head * HD : (head + 1) * HD] = attended[head * new_rows : (head + 1) * new_rows]
+    fetch.wait()
+    shift = length - start
+    fresh = group_ref[:, per_group * HD :].astype(jnp.float32)
+    fresh = jnp.concatenate([fresh, jnp.zeros((tile, 2 * HD), jnp.float32)], axis=0)
+    fresh = pltpu.roll(fresh, shift, 0)
+    row_at = lax.broadcasted_iota(jnp.int32, fresh.shape, 0)
+    replaced = jnp.logical_and(row_at >= shift, row_at < shift + new_rows)
+    window = jnp.where(replaced, fresh, window_ref[...].astype(jnp.float32))
+    window_ref[...] = window.astype(window_ref.dtype)
+    store = pltpu.make_async_copy(
+        window_ref, appended_ref.at[pl.ds(start, window_rows)], window_sem
+    )
+    store.start()
+    store.wait()
+
+
+def attend_call(places, lengths, requests, group_cols, cache_rows):
+    new_rows = group_cols.shape[0]
+    query_rows = HEADS // KVH * new_rows
+    cache_len = cache_rows.shape[0]
+    block_len = min(512, cache_len)
+    vmem = pl.BlockSpec(memory_space=pltpu.VMEM)
+    anywhere = pl.BlockSpec(memory_space=pl.ANY)
+    return pl.pallas_call(
+        attend_kernel,
+        out_shape=[
+            jax.ShapeDtypeStruct((new_rows, HEADS // KVH * HD), jnp.bfloat16),
+            jax.ShapeDtypeStruct(cache_rows.shape, cache_rows.dtype),
+        ],
+        in_specs=[pl.BlockSpec(memory_space=pltpu.SMEM)] * 3 + [vmem, anywhere],
+        out_specs=[vmem, anywhere],
+        scratch_shapes=[
+            pltpu.VMEM((cache_len // block_len, block_len, 2 * HD), jnp.bfloat16),
+            pltpu.VMEM((new_rows + 16, 2 * HD), jnp.bfloat16),
+            pltpu.VMEM((HD, query_rows), jnp.float32),
+            pltpu.VMEM((1, query_rows), jnp.float32),
+            pltpu.VMEM((1, query_rows), jnp.float32),
+            pltpu.SemaphoreType.DMA((cache_len // block_len,)),
+            pltpu.SemaphoreType.DMA,
+            pltpu.SemaphoreType.DMA,
+        ],
+        compiler_params=pltpu.CompilerParams(vmem_limit_bytes=24 * 1024 * 1024),
+        cost_estimate=pl.CostEstimate(
+            flops=4 * query_rows * cache_len * HD,
+            bytes_accessed=4 * cache_rows.size,
+            transcendentals=query_rows * cache_len,
+        ),
+    )(places, lengths, requests, group_cols, cache_rows)
+
+
+def project_near_kernel(place_ref, *refs):
+    piece_refs, gain_ref, weights = refs[:8], refs[8], refs[9:11]
+    normed_ref, out_ref = refs[11:]
+    gy_place, z_place, x_place = (place_ref[at] for at in range(3))
+    rows, width = piece_refs[0].shape
+    squares = jnp.zeros((rows, width), jnp.float32)
+    for piece_ref in piece_refs:
+        values = piece_ref[...].astype(jnp.float32)
+        squares = squares + values * values
+    mean_square = jnp.sum(squares, axis=1, keepdims=True) / (len(piece_refs) * width)
+    factor = lax.rsqrt(mean_square + epsilon)
+    for (far, near), piece_ref in zip(PAIRS, piece_refs):
+        block, half = z_place ^ far, x_place ^ near
+        values = piece_ref[...].astype(jnp.float32) * factor
+        values = values * gain_ref[2 * block + half].astype(jnp.float32)
+        normed_ref[block, half] = values.astype(jnp.bfloat16)
+    total = jnp.zeros(out_ref.shape, jnp.float32)
+    for offset, weight in enumerate(weights):
+        for half in range(2):
+            total = total + jnp.dot(
+                normed_ref[gy_place ^ offset, half],
+                weight[half * width : (half + 1) * width],
+                preferred_element_type=jnp.float32,
+            )
+    out_ref[...] = total
+
+
+def project_far_kernel(place_ref, normed_ref, near_ref, far, far_near, out_ref):
+    width = normed_ref.shape[3]
+    total = near_ref[...]
+    for offset, weight in ((2, far), (3, far_near)):
+        for half in range(2):
+            total = total + jnp.dot(
+                normed_ref[place_ref[0] ^ offset, half],
+                weight[half * width : (half + 1) * width],
+                preferred_element_type=jnp.float32,
+            )
+    out_ref[...] = total.astype(out_ref.dtype)
+
+
+SMEM = pl.BlockSpec(memory_space=pltpu.SMEM)
+VMEM = pl.BlockSpec(memory_space=pltpu.VMEM)
+ANYWHERE = pl.BlockSpec(memory_space=pl.ANY)
+
+
+def project_near_call(places, pieces, gain, own, near):
+    rows, width = pieces[0].shape
+    depth, columns = own.shape
+    return pl.pallas_call(
+        project_near_kernel,
+        out_shape=[
+            jax.ShapeDtypeStruct((4, 2, rows, width), jnp.bfloat16),
+            jax.ShapeDtypeStruct((rows, columns), jnp.float32),
+        ],
+        in_specs=[SMEM] + [VMEM] * 11,
+        out_specs=[VMEM] * 2,
+        compiler_params=pltpu.CompilerParams(vmem_limit_bytes=24 * 1024 * 1024),
+        cost_estimate=pl.CostEstimate(
+            flops=4 * rows * depth * columns,
+            bytes_accessed=4 * depth * columns,
+            transcendentals=rows,
+        ),
+    )(places, *pieces, gain.reshape(len(pieces), 1, width), own, near)
+
+
+def project_far_call(places, normed, near, far_weights):
+    rows, columns = near.shape
+    depth = far_weights[0].shape[0]
+    return pl.pallas_call(
+        project_far_kernel,
+        out_shape=jax.ShapeDtypeStruct((rows, columns), jnp.bfloat16),
+        in_specs=[SMEM] + [VMEM] * 4,
+        out_specs=VMEM,
+        compiler_params=pltpu.CompilerParams(vmem_limit_bytes=24 * 1024 * 1024),
+        cost_estimate=pl.CostEstimate(
+            flops=4 * rows * depth * columns,
+            bytes_accessed=4 * depth * columns,
+            transcendentals=0,
+        ),
+    )(places, normed, near, *far_weights)
+
+
+def out_kernel(place_ref, attended_ref, weight_ref, *out_refs):
+    z_place, x_place = place_ref[1], place_ref[2]
+    width = out_refs[0].shape[1]
+    for (far, near), out_ref in zip(PAIRS, out_refs):
+        column = pl.multiple_of((x_place ^ near) * width, width)
+        out_ref[...] = jnp.dot(
+            attended_ref[z_place ^ far],
+            weight_ref[:, pl.ds(column, width)],
+            preferred_element_type=jnp.float32,
+        ).astype(out_ref.dtype)
+
+
+def out_call(places, attended, weight):
+    slots, rows, depth = attended.shape
+    columns = weight.shape[1]
+    piece = jax.ShapeDtypeStruct((rows, columns // 2), jnp.bfloat16)
+    return pl.pallas_call(
+        out_kernel,
+        out_shape=[piece] * 8,
+        in_specs=[SMEM, VMEM, VMEM],
+        out_specs=[VMEM] * 8,
+        compiler_params=pltpu.CompilerParams(vmem_limit_bytes=16 * 1024 * 1024),
+        cost_estimate=pl.CostEstimate(
+            flops=2 * slots * rows * depth * columns,
+            bytes_accessed=2 * depth * columns,
+            transcendentals=0,
+        ),
+    )(places, attended, weight)
+
+
+def up_kernel(place_ref, *refs):
+    sources, gain_ref, weight_source = refs[:8], refs[8], refs[9]
+    sent_ref, kept_ref, last_ref, scaled_ref, piece_ref, weight_ref, sems = refs[10:]
+    copies = [
+        pltpu.make_async_copy(source, piece_ref.at[at], sems.at[at])
+        for at, source in enumerate(sources)
+    ]
+    copies.append(pltpu.make_async_copy(weight_source, weight_ref, sems.at[len(sources)]))
+    for copy in copies:
+        copy.start()
+    gy_place, z_place, x_place = (place_ref[at] for at in range(3))
+    core = gy_place % 2
+    rows, width = piece_ref.shape[1:]
+    columns = weight_ref.shape[1]
+    ones = jnp.ones((8, width), jnp.float32)
+    for far in range(4):
+        slot = z_place ^ far
+        squares = jnp.zeros((rows, width), jnp.float32)
+        for near in range(2):
+            half = x_place ^ near
+            copies[2 * far + near].wait()
+            values = piece_ref[2 * far + near].astype(jnp.float32)
+            squares = squares + values * values
+            gain = gain_ref[:, pl.ds(pl.multiple_of(half * width, width), width)]
+            scaled_ref[slot % 2, half, slot // 2] = (values * gain).astype(jnp.bfloat16)
+        sums = lax.dot_general(
+            ones,
+            squares,
+            (((1,), (1,)), ((), ())),
+            precision=lax.Precision.HIGHEST,
+            preferred_element_type=jnp.float32,
+        )
+        last_ref[slot, :, columns:] = sums[:1]
+    copies[-1].wait()
+    step = 512
+    for parity, out_ref in ((1 - core, sent_ref), (core, kept_ref)):
+        for column in range(0, columns, step):
+            total = jnp.zeros((2 * rows, step), jnp.float32)
+            for half in range(2):
+                total = total + jnp.dot(
+                    scaled_ref[parity, half].reshape(2 * rows, width),
+                    weight_ref[half * width : (half + 1) * width, column : column + step],
+                    preferred_element_type=jnp.float32,
+                )
+            for pair in range(2):
+                last_row = total[(pair + 1) * rows - 1 : (pair + 1) * rows]
+                last_ref[2 * pair + parity, :, column : column + step] = last_row
+            out_ref[:, :, column : column + step] = total.reshape(2, rows, step).astype(
+                out_ref.dtype
+            )
+
+
+def up_call(places, pieces, gain, weight):
+    rows, width = pieces[0].shape
+    depth, columns = weight.shape
+    return pl.pallas_call(
+        up_kernel,
+        out_shape=[
+            jax.ShapeDtypeStruct((2, rows, columns), jnp.bfloat16),
+            jax.ShapeDtypeStruct((2, rows, columns), jnp.float32),
+            jax.ShapeDtypeStruct((4, 1, columns + rows), jnp.float32),
+        ],
+        in_specs=[SMEM] + [ANYWHERE] * 8 + [VMEM, ANYWHERE],
+        out_specs=[VMEM] * 3,
+        scratch_shapes=[
+            pltpu.VMEM((2, 2, 2, rows, width), jnp.bfloat16),
+            pltpu.VMEM((8, rows, width), jnp.bfloat16),
+            pltpu.VMEM((depth, columns), jnp.bfloat16),
+            pltpu.SemaphoreType.DMA((9,)),
+        ],
+        compiler_params=pltpu.CompilerParams(vmem_limit_bytes=48 * 1024 * 1024),
+        cost_estimate=pl.CostEstimate(
+            flops=8 * rows * depth * columns,
+            bytes_accessed=2 * depth * columns,
+            transcendentals=0,
+        ),
+    )(places, *pieces, gain.reshape(1, depth), weight)
+
+
+def down_kernel(place_ref, active_ref, *refs):
+    sources, out_refs, tie_ref, (weight_ref, sems) = refs[:4], refs[4:12], refs[12], refs[13:]
+    gy_place, z_place, x_place = (place_ref[at] for at in range(3))
+    copies = [
+        pltpu.make_async_copy(source, weight_ref.at[at], sems.at[at])
+        for at, source in enumerate(sources)
+    ]
+    for copy in copies:
+        copy.start()
+    width = out_refs[0].shape[1]
+    for copy in copies:
+        copy.wait()
+    for (far, near), out_ref in zip(PAIRS, out_refs):
+        offset = gy_place ^ z_place ^ far
+        column = pl.multiple_of((x_place ^ near) * width, width)
+        out_ref[...] = jnp.dot(
+            active_ref[...],
+            weight_ref[offset, :, pl.ds(column, width)],
+            preferred_element_type=jnp.float32,
+        ).astype(out_ref.dtype)
+    tie_ref[...] = jnp.zeros_like(tie_ref)
+
+
+def down_call(places, active, weights):
+    rows, hidden = active.shape
+    columns = weights[0].shape[1]
+    piece = jax.ShapeDtypeStruct((rows, columns // 2), jnp.bfloat16)
+    *pieces, tie = pl.pallas_call(
+        down_kernel,
+        out_shape=[piece] * 8 + [jax.ShapeDtypeStruct((8, 128), jnp.float32)],
+        in_specs=[SMEM, VMEM] + [ANYWHERE] * 4,
+        out_specs=[VMEM] * 9,
+        scratch_shapes=[
+            pltpu.VMEM((4, hidden, columns), jnp.bfloat16),
+            pltpu.SemaphoreType.DMA((4,)),
+        ],
+        compiler_params=pltpu.CompilerParams(vmem_limit_bytes=32 * 1024 * 1024),
+        cost_estimate=pl.CostEstimate(
+            flops=8 * rows * hidden * columns,
+            bytes_accessed=8 * hidden * columns,
+            transcendentals=0,
+        ),
+    )(places, active, *weights)
+    return pieces, tie
+
+
+def head_kernel(rows_ref, weight_ref, out_ref):
+    logits = jnp.dot(rows_ref[...], weight_ref[...], preferred_element_type=jnp.float32)
+
+    @pl.when(pl.program_id(0) == 0)
+    def _():
+        out_ref[...] = logits
+
+    @pl.when(pl.program_id(0) > 0)
+    def _():
+        out_ref[...] = jnp.maximum(out_ref[...], logits)
+
+
+def head_call(head_rows, weight, part):
+    depth, columns = weight.shape
+    step = min(512, columns // 2)
+    count = columns // 2 // step
+    return pl.pallas_call(
+        head_kernel,
+        grid=(count,),
+        out_shape=jax.ShapeDtypeStruct((head_rows.shape[0], step), jnp.float32),
+        in_specs=[
+            pl.BlockSpec(head_rows.shape, lambda at: (0, 0)),
+            pl.BlockSpec((depth, step), lambda at: (0, part * count + at)),
+        ],
+        out_specs=pl.BlockSpec((head_rows.shape[0], step), lambda at: (0, 0)),
+        compiler_params=pltpu.CompilerParams(vmem_limit_bytes=24 * 1024 * 1024),
+        cost_estimate=pl.CostEstimate(
+            flops=head_rows.shape[0] * depth * columns,
+            bytes_accessed=depth * columns,
+            transcendentals=0,
+        ),
+    )(head_rows, weight)
+
+
+def stationary(
+    tokens,
+    attn_gain,
+    qkv_weight,
+    out_weight,
+    mlp_gain,
+    up_weight,
+    down_weight,
+    final_gain,
+    head_weight,
+    kv_cache,
+    cache_lengths,
+    slot_request,
+):
+    gx_count = lax.axis_size("gx")
+    gy_count = lax.axis_size("gy")
+    device_count = gx_count * gy_count
+    gx_place, gy_place = lax.axis_index("gx"), lax.axis_index("gy")
+    z_place, x_place, pair_place = gx_place // 2, gx_place % 2, gy_place // 2
+    places = jnp.stack([gy_place, z_place, x_place])
+    rows, width = tokens.shape
+    features = gx_count * width
+    own_features, hidden_units = up_weight.shape
+
+    def pick(blocks, place):
+        return lax.dynamic_index_in_dim(blocks, place, 0, keepdims=False)
+
+    def to_all(block):
+        pieces = jnp.broadcast_to(block[None], (device_count,) + block.shape)
+        return exchange(pieces, ("gx", "gy")).reshape((gx_count, gy_count) + block.shape)
+
+    far_qkv = xor_permute(qkv_weight, "gy", 2)
+    near_qkv = xor_permute(qkv_weight, "gy", 1)
+    normed, near_terms = project_near_call(
+        places, gather_blocks(tokens), attn_gain, qkv_weight, near_qkv
+    )
+    far_qkv, normed, near_terms = lax.optimization_barrier((far_qkv, normed, near_terms))
+    far_weights = (far_qkv, xor_permute(far_qkv, "gy", 1))
+    group_cols = project_far_call(places, normed, near_terms, far_weights)
+    held = transpose_places(tokens)
+
+    attended, appended = attend_call(
+        places, cache_lengths, slot_request, group_cols, kv_cache[0]
+    )
+    new_cache = appended[None]
+
+    attended, held = lax.optimization_barrier((attended, held))
+    attention = lax.all_gather(attended, "gy", axis=0)
+    sent_weight, attention = lax.optimization_barrier((down_weight, attention))
+    far_down = xor_permute(sent_weight, "gy", 2)
+    near_down = xor_permute(down_weight, "gy", 1)
+
+    middle = held.astype(jnp.float32) + scatter_blocks(out_call(places, attention, out_weight))
+    middle = middle.astype(jnp.bfloat16)
+
+    gain = lax.dynamic_slice_in_dim(mlp_gain, gy_place * own_features, own_features, 0)
+    blocks = gather_blocks(middle)
+    sent, kept, last_up = up_call(places, blocks, gain.astype(jnp.float32), up_weight)
+    moved, _ = lax.optimization_barrier((middle, blocks[-1]))
+    middle_slot = transpose_places(moved)
+    received = xor_permute(sent, "gy", 1)
+    last_up = last_up[:, 0]
+    last_up = last_up + xor_permute(last_up, "gy", 1)
+    other = pick(kept, 1 - pair_place) + pick(received, 1 - pair_place).astype(jnp.float32)
+    other, last_up, middle_slot = lax.optimization_barrier(
+        (other.astype(jnp.bfloat16), last_up, middle_slot)
+    )
+    far_down, _ = lax.optimization_barrier((far_down, other))
+    far_near_down = xor_permute(far_down, "gy", 1)
+    far_up = xor_permute(other, "gy", 2)
+    last_up = last_up + xor_permute(last_up, "gy", 2)
+    factors = lax.rsqrt(last_up[:, hidden_units:] / features + epsilon)
+
+    last_active = jnp.maximum(last_up[:, :hidden_units] * factors[:, rows - 1 :], 0.0)
+    last_terms = rows_dot((last_active * last_active).astype(jnp.bfloat16), down_weight)
+    last_row = middle[rows - 1 :].astype(jnp.float32)
+    blank = jnp.zeros_like(last_terms)
+    last_terms = last_terms + lax.dynamic_update_slice(
+        blank, last_row, (z_place, x_place * width)
+    )
+    last_pieces = to_all(last_terms.astype(jnp.bfloat16))
+
+    up_values = pick(kept, pair_place) + pick(received, pair_place).astype(jnp.float32)
+    up_values = up_values + far_up.astype(jnp.float32)
+    rectified = jnp.maximum(up_values * pick(factors, gy_place)[:, None], 0.0)
+    activation = (rectified * rectified).astype(jnp.bfloat16)
+    down_weights = (down_weight, near_down, far_down, far_near_down)
+    pieces, tie = down_call(places, activation, down_weights)
+    last_pieces, _ = lax.optimization_barrier((last_pieces, tie))
+    last_hidden = jnp.sum(last_pieces.astype(jnp.float32), axis=0)
+    last_hidden = last_hidden.transpose(1, 0, 2).reshape(gy_count, features)
+    last_hidden = last_hidden.astype(jnp.bfloat16).astype(jnp.float32)
+    mean_square = jnp.mean(last_hidden * last_hidden, axis=1)
+    last_norms = jnp.sqrt(mean_square)
+    head_input = (
+        last_hidden * lax.rsqrt(mean_square + epsilon)[:, None] * final_gain.astype(jnp.float32)
+    ).astype(jnp.bfloat16)
+    first_max = head_call(head_input, head_weight, 0)
+    second_max = head_call(head_input, head_weight, 1)
+    largest = jnp.max(jnp.maximum(first_max, second_max), axis=1)
+    max_logits = jnp.max(to_all(largest), axis=(0, 1))
+
+    hidden_terms = scatter_blocks(pieces, first_max)
+    hidden_out = (middle_slot.astype(jnp.float32) + hidden_terms).astype(jnp.bfloat16)
+    return (hidden_out, new_cache, last_norms, max_logits, head_input)
+
+
 def solution(mesh):
+    gx_count, gy_count = mesh.shape["gx"], mesh.shape["gy"]
+    body = stationary if gx_count == KVH and gy_count == 4 else local
     in_specs = (
         P("gy", "gx"),
         P(),
@@ -212,4 +801,4 @@
         P(),
     )
     out_specs = (P("gy", "gx"), P(("gy", "gx"), None, None), P(), P(), P())
-    return jax.shard_map(local, mesh=mesh, in_specs=in_specs, out_specs=out_specs, check_vma=False)
+    return jax.shard_map(body, mesh=mesh, in_specs=in_specs, out_specs=out_specs, check_vma=False)

time: 588 us -> 206 us (0.35)
  waiting for transfers between devices: 440 us -> 77.6 us
  blocking collectives: 76.6 us -> 17.3 us
  starting transfers between devices: 0.31 us -> 52.3 us
  Pallas kernels: 0 us -> 39.3 us
  matrix products: 38.1 us -> 0.55 us
  between operations: 19 us -> 0.99 us
    all_gather x6 -> x0, waiting for transfers between devices: 311 us -> none  [the longest x2 126 us: rows_product(): lax.all_gather(weight_shard, 'gy', axis=0, tiled=True)]
    reduce_scatter x2 -> x0, waiting for transfers between devices: 125 us -> none  [scatter_partials(): lax.psum_scatter(partial_terms.astype(jnp.bfloat16), 'gx', scatter_dimens...]
    ppermute x0 -> x40, waiting for transfers between devices: none -> 72 us  [the longest x38 72 us: xor_permute(): lax.ppermute(values, axis, [(place, place ^ distance) for place in range(...]
    ppermute x0 -> x40, starting transfers between devices: none -> 46.9 us  [the longest x38 44.7 us: xor_permute(): lax.ppermute(values, axis, [(place, place ^ distance) for place in range(...]
    pallas_call x0 -> x8, Pallas kernels: none -> 39.3 us  [the longest x2 14.4 us: head_call(): pl.pallas_call(head_kernel, grid=(count,), out_shape=jax.ShapeDtypeStruct...]
    dot_general x10 -> x1, matrix products: 38.1 us -> 0.55 us  [rows_dot(): lax.dot_general(left, weight, (((left.ndim - 1,), (0,)), ((), ())), prefe...]
    pmax x1 -> x0, blocking collectives: 36.9 us -> none  [local(): max_logits = lax.pmax(jnp.max(logits, axis=1), ('gx', 'gy'))]
    all_gather x1, blocking collectives: 39.7 us -> 7.81 us  [stationary(): attention = lax.all_gather(attended, 'gy', axis=0)]
  transfers between devices with their start and end apart: 8 -> 41, of which waited for: 8 -> 21; matrix products, arithmetic and copies ran while one was open for 3% -> 6% of each run, Pallas kernels for 0% -> 16%
where the time goes in v1:
time: 206 us
  waiting for transfers between devices  77.6 us (38%)
  starting transfers between devices  52.3 us (25%)
  Pallas kernels  39.3 us (19%)
  blocking collectives  17.3 us (8%)
  other arithmetic  10.8 us (5%)
  local copies, waits for them, and re-layouts  6.76 us (3%)
    ppermute x38, waiting for transfers between devices, xor_permute(): lax.ppermute(values, axis, [(place, place ^ distance) for place in range(...  72 us
    ppermute x38, starting transfers between devices, xor_permute(): lax.ppermute(values, axis, [(place, place ^ distance) for place in range(...  44.7 us
    pallas_call x2, Pallas kernels, head_call(): pl.pallas_call(head_kernel, grid=(count,), out_shape=jax.ShapeDtypeStruct...  14.4 us
    all_to_all x1, blocking collectives, exchange(): return lax.all_to_all(blocks, axes, split_axis=0, concat_axis=0, tiled=True)  9.52 us
    all_gather x1, blocking collectives, stationary(): attention = lax.all_gather(attended, 'gy', axis=0)  7.81 us
    pallas_call x1, Pallas kernels, attend_call(): pl.pallas_call(attend_kernel, out_shape=[jax.ShapeDtypeStruct((new_rows,...  7.62 us
    pallas_call x1, Pallas kernels, down_call(): pl.pallas_call(down_kernel, out_shape=[piece] * 8 + [jax.ShapeDtypeStruct...  6.85 us
    pallas_call x1, Pallas kernels, up_call(): pl.pallas_call(up_kernel, out_shape=[jax.ShapeDtypeStruct((2, rows, colum...  5.74 us
  transfers between devices with their start and end apart: 41, of which 21 were waited for; matrix products, arithmetic and copies ran while one was open for 6% of the time, Pallas kernels for 16%

profile of v1, /device:TPU:0, one launch (start us, length us, event | category | flops | bytes accessed | tf_op | source)
XLA Modules:
  0.0 205.6 jit_solution(6364076270718438797)
XLA Ops:
  1.1 2.6 %collective-permute-start = (bf16[1024,768]{1,0:T(8,128)(2,1)}, bf16[1024,768]{1,0:T(8,128)(2,1)S(1)}, u32[]{:S(2)}, u32[]{:S(2)}) collective-permute-start(bf16[1024,768]{1,0:T(8,128)(2,1)} %refs_9_.2), channel_id=1, source_target_pairs={{0,2},{1,3},{2,0},{3,1},{4,6},{5,7},{6,4},{7,5},{8,10},{9,11},{10,... | collective-permute-start | bytes 4718600 | tf_op jit(solution)/shard_map/ppermute | solution.py:203
  3.7 3.6 %collective-permute-start.6 = (bf16[128,512]{1,0:T(8,128)(2,1)}, bf16[128,512]{1,0:T(8,128)(2,1)S(1)}, u32[]{:S(2)}, u32[]{:S(2)}) collective-permute-start(bf16[128,512]{1,0:T(8,128)(2,1)} %refs_0_.2), channel_id=1, source_target_pairs={{0,24},{4,28},{8,16},{12,20},{16,8},{20,12},{24,0},{28,4},{1,25},{... | collective-permute-start | bytes 393224 | tf_op jit(solution)/shard_map/ppermute | solution.py:203
  8.1 4.1 %collective-permute-done.6.refs_6_ = bf16[128,512]{1,0:T(8,128)(2,1)S(1)} collective-permute-done((bf16[128,512]{1,0:T(8,128)(2,1)}, bf16[128,512]{1,0:T(8,128)(2,1)S(1)}, u32[]{:S(2)}, u32[]{:S(2)}) %collective-permute-start.6) | collective-permute-done | bytes 131104 | tf_op jit(solution)/shard_map/ppermute | solution.py:203
  13.7 5.3 %collective-permute-done.4.refs_4_ = bf16[128,512]{1,0:T(8,128)(2,1)S(1)} collective-permute-done((bf16[128,512]{1,0:T(8,128)(2,1)}, bf16[128,512]{1,0:T(8,128)(2,1)S(1)}, u32[]{:S(2)}, u32[]{:S(2)}) %collective-permute-start.4) | collective-permute-done | bytes 131104 | tf_op jit(solution)/shard_map/ppermute | solution.py:203
  25.5 2.5 %collective-permute-done.5.refs_5_ = bf16[128,512]{1,0:T(8,128)(2,1)} collective-permute-done((bf16[128,512]{1,0:T(8,128)(2,1)S(1)}, bf16[128,512]{1,0:T(8,128)(2,1)}, u32[]{:S(2)}, u32[]{:S(2)}) %collective-permute-start.5) | collective-permute-done | bytes 131104 | tf_op jit(solution)/shard_map/ppermute | solution.py:203
  31.7 2.3 %shard_map.155 = (bf16[4,2,128,512]{3,2,1,0:T(8,128)(2,1)S(1)}, f32[128,768]{1,0:T(8,128)S(1)}) custom-call(s32[3]{0:T(128)S(1)} %pad_add_fusion.place_ref, bf16[128,512]{1,0:T(8,128)(2,1)} %refs_0_.2, bf16[128,512]{1,0:T(8,128)(2,1)S(1)} %copy-done.5, bf16[128,512]{1,0:T(8,128)(2,1)S(1)} %collective-permute-done.2.refs_2_, ...), custom_call_target="tpu_custom_call" | custom-call | flops 402653184 | bytes 3145728 | tf_op jit(solution)/shard_map/pallas_call | solution.py:456
  34.0 4.9 %collective-permute-done.far = bf16[1024,768]{1,0:T(8,128)(2,1)S(1)} collective-permute-done((bf16[1024,768]{1,0:T(8,128)(2,1)}, bf16[1024,768]{1,0:T(8,128)(2,1)S(1)}, u32[]{:S(2)}, u32[]{:S(2)}) %collective-permute-start) | collective-permute-done | bytes 1572896 | tf_op jit(solution)/shard_map/ppermute | solution.py:203
  43.5 7.6 %shard_map.157 = (bf16[128,512]{1,0:T(8,128)(2,1)S(1)}, bf16[4096,256]{1,0:T(8,128)(2,1)}) custom-call(s32[3]{0:T(128)S(1)} %pad_add_fusion.place_ref, s32[4]{0:T(128)S(1)} %copy-done.13, s32[4]{0:T(128)S(1)} %copy-done.14, bf16[128,768]{1,0:T(8,128)(2,1)S(1)} %shard_map.156.group_ref, bf16[4096,256]{1,0:T(8,128)(2,1)S(1)} %bitcast.33), custom_call_target="tpu_custom_call" | custom-call | flops 1073741824 | bytes 4194304 | tf_op jit(solution)/shard_map/pallas_call | solution.py:381
  51.2 7.8 %all-gather = bf16[512,512]{1,0:T(8,128)(2,1)S(1)} all-gather(bf16[128,512]{1,0:T(8,128)(2,1)S(1)} %get-tuple-element.49), channel_id=2, replica_groups=mesh['gx'=8,'gy'=4] {'gy'}, dimensions={0}, use_global_device_ids=true | all-gather | bytes 655360 | tf_op jit(solution)/shard_map/all_gather | solution.py:726
  68.4 6.7 %collective-permute-done.16 = bf16[128,512]{1,0:T(8,128)(2,1)S(1)} collective-permute-done((bf16[128,512]{1,0:T(8,128)(2,1)S(1)}, bf16[128,512]{1,0:T(8,128)(2,1)S(1)}, u32[]{:S(2)}, u32[]{:S(2)}) %collective-permute-start.16) | collective-permute-done | bytes 131104 | tf_op jit(solution)/shard_map/ppermute | solution.py:203
  78.5 8.4 %collective-permute-done.15 = bf16[128,512]{1,0:T(8,128)(2,1)S(1)} collective-permute-done((bf16[128,512]{1,0:T(8,128)(2,1)S(1)}, bf16[128,512]{1,0:T(8,128)(2,1)S(1)}, u32[]{:S(2)}, u32[]{:S(2)}) %collective-permute-start.15) | collective-permute-done | bytes 131104 | tf_op jit(solution)/shard_map/ppermute | solution.py:203
  95.4 6.6 %collective-permute-done.21.refs_4_ = bf16[128,512]{1,0:T(8,128)(2,1)} collective-permute-done((bf16[128,512]{1,0:T(8,128)(2,1)S(1)}, bf16[128,512]{1,0:T(8,128)(2,1)}, u32[]{:S(2)}, u32[]{:S(2)}) %collective-permute-start.21) | collective-permute-done | bytes 131104 | tf_op jit(solution)/shard_map/ppermute | solution.py:203
  104.7 4.0 %collective-permute-done.22.refs_5_ = bf16[128,512]{1,0:T(8,128)(2,1)} collective-permute-done((bf16[128,512]{1,0:T(8,128)(2,1)}, bf16[128,512]{1,0:T(8,128)(2,1)}, u32[]{:S(2)}, u32[]{:S(2)}) %collective-permute-start.22) | collective-permute-done | bytes 131104 | tf_op jit(solution)/shard_map/ppermute | solution.py:203
  111.0 5.7 %shard_map.159 = (bf16[2,128,1536]{2,1,0:T(8,128)(2,1)}, f32[2,128,1536]{2,1,0:T(8,128)S(1)}, f32[4,1,1664]{2,1,0:T(1,128)S(1)}) custom-call(s32[3]{0:T(128)S(1)} %copy-done.9, bf16[128,512]{1,0:T(8,128)(2,1)S(1)} %add_convert_fusion.4.refs_0_, bf16[128,512]{1,0:T(8,128)(2,1)} %collective-permute-done.18.refs_1_, ...), custom_call_target="tpu_custom_call" | custom-call | flops 1610612736 | bytes 3145728 | tf_op jit(solution)/shard_map/pallas_call | solution.py:575
  122.9 7.6 %collective-permute-done.31.refs_2_ = bf16[1536,1024]{1,0:T(8,128)(2,1)} collective-permute-done((bf16[1536,1024]{1,0:T(8,128)(2,1)S(1)}, bf16[1536,1024]{1,0:T(8,128)(2,1)}, u32[]{:S(2)}, u32[]{:S(2)}) %collective-permute-start.31) | collective-permute-done | bytes 3145760 | tf_op jit(solution)/shard_map/ppermute | solution.py:203
  130.5 2.6 %collective-permute-start.29 = (f32[4,1664]{1,0:T(4,128)S(1)}, f32[4,1664]{1,0:T(4,128)S(1)}, u32[]{:S(2)}, u32[]{:S(2)}) collective-permute-start(f32[4,1664]{1,0:T(4,128)S(1)} %fusion.17), channel_id=1, source_target_pairs={{0,2},{1,3},{2,0},{3,1},{4,6},{5,7},{6,4},{7,5},{8,10},{9,11},{10,... | collective-permute-start | bytes 79880 | tf_op jit(solution)/shard_map/ppermute | solution.py:203
  136.9 5.4 %all-to-all-start = ((bf16[32,4,1024]{2,1,0:T(4,128)(2,1)}), bf16[32,4,1024]{2,1,0:T(4,128)(2,1)}, u32[]{:S(2)}, u32[]{:S(2)}) async-start(bf16[32,4,1024]{2,1,0:T(4,128)(2,1)} %broadcast_in_dim.6), calls=%async_computation | async-start | bytes 524288 | tf_op jit(solution)/shard_map/all_to_all | solution.py:218
  142.3 3.2 %collective-permute-done.28 = bf16[128,1536]{1,0:T(8,128)(2,1)} collective-permute-done((bf16[128,1536]{1,0:T(8,128)(2,1)}, bf16[128,1536]{1,0:T(8,128)(2,1)}, u32[]{:S(2)}, u32[]{:S(2)}) %collective-permute-start.28) | collective-permute-done | bytes 393248 | tf_op jit(solution)/shard_map/ppermute | solution.py:203
  147.0 5.7 %all-to-all-done = bf16[32,4,1024]{2,1,0:T(4,128)(2,1)} async-done(((bf16[32,4,1024]{2,1,0:T(4,128)(2,1)}), bf16[32,4,1024]{2,1,0:T(4,128)(2,1)}, u32[]{:S(2)}, u32[]{:S(2)}) %all-to-all-start) | async-done | bytes 262176 | tf_op jit(solution)/shard_map/all_to_all | solution.py:218
  156.6 6.9 %shard_map.160 = (bf16[128,512]{1,0:T(8,128)(2,1)S(1)}, bf16[128,512]{1,0:T(8,128)(2,1)}, bf16[128,512]{1,0:T(8,128)(2,1)}, bf16[128,512]{1,0:T(8,128)(2,1)}, bf...) custom-call(s32[3]{0:T(128)S(1)} %copy-done.10, ...), custom_call_target="tpu_custom_call" | custom-call | flops 1610612736 | bytes 12582912 | tf_op jit(solution)/shard_map/pallas_call | solution.py:626
  164.5 7.2 %shard_map.161 = f32[4,512]{1,0:T(4,128)S(1)} custom-call(bf16[4,4096]{1,0:T(4,128)(2,1)S(1)} %multiply_convert_fusion.rows_ref, bf16[4096,4096]{1,0:T(8,128)(2,1)} %weight_ref.5), custom_call_target="tpu_custom_call" | custom-call | flops 67108864 | bytes 16777216 | tf_op jit(solution)/shard_map/pallas_call | solution.py:661
  176.4 8.2 %collective-permute-done.37 = bf16[128,512]{1,0:T(8,128)(2,1)S(1)} collective-permute-done((bf16[128,512]{1,0:T(8,128)(2,1)S(1)}, bf16[128,512]{1,0:T(8,128)(2,1)S(1)}, u32[]{:S(2)}, u32[]{:S(2)}) %collective-permute-start.37) | collective-permute-done | bytes 131104 | tf_op jit(solution)/shard_map/ppermute | solution.py:203
  187.3 7.2 %shard_map.162 = f32[4,512]{1,0:T(4,128)S(1)} custom-call(bf16[4,4096]{1,0:T(4,128)(2,1)S(1)} %multiply_convert_fusion.rows_ref, bf16[4096,4096]{1,0:T(8,128)(2,1)} %weight_ref.5), custom_call_target="tpu_custom_call" | custom-call | flops 67108864 | bytes 16777216 | tf_op jit(solution)/shard_map/pallas_call | solution.py:661
  194.7 9.5 %all_to_all.11 = f32[32,1,4]{2,1,0:T(1,128)S(1)} all-to-all(f32[32,1,4]{2,1,0:T(1,128)S(1)} %broadcast_in_dim.8), channel_id=1, replica_groups=mesh['gx'=8,'gy'=4] {'gx','gy'}, dimensions={0} | all-to-all | bytes 1024 | tf_op jit(solution)/shard_map/all_to_all | solution.py:218
  (137 shorter events, 69.3 us)
Async XLA Ops:
  0.6 28.8 %collective-permute-start.8 = (bf16[1024,768]{1,0:T(8,128)(2,1)}, bf16[1024,768]{1,0:T(8,128)(2,1)S(1)}, u32[]{:S(2)}, u32[]{:S(2)}) collective-permute-start(bf16[1024,768]{1,0:T(8,128)(2,1)} %refs_9_.2), channel_id=1, source_target_pairs={{0,1},{1,0},{2,3},{3,2},{4,5},{5,4},{6,7},{7,6},{8,9},{9,8},{10,11... | collective-permute-start | bytes 4718600 | tf_op jit(solution)/shard_map/ppermute | solution.py:203
  1.1 37.8 %collective-permute-start = (bf16[1024,768]{1,0:T(8,128)(2,1)}, bf16[1024,768]{1,0:T(8,128)(2,1)S(1)}, u32[]{:S(2)}, u32[]{:S(2)}) collective-permute-start(bf16[1024,768]{1,0:T(8,128)(2,1)} %refs_9_.2), channel_id=1, source_target_pairs={{0,2},{1,3},{2,0},{3,1},{4,6},{5,7},{6,4},{7,5},{8,10},{9,11},{10,... | collective-permute-start | bytes 4718600 | tf_op jit(solution)/shard_map/ppermute | solution.py:203
  7.3 11.6 %collective-permute-start.4 = (bf16[128,512]{1,0:T(8,128)(2,1)}, bf16[128,512]{1,0:T(8,128)(2,1)S(1)}, u32[]{:S(2)}, u32[]{:S(2)}) collective-permute-start(bf16[128,512]{1,0:T(8,128)(2,1)} %refs_0_.2), channel_id=1, source_target_pairs={{0,16},{4,20},{8,24},{12,28},{16,0},{20,4},{24,8},{28,12},{1,17},{... | collective-permute-start | bytes 393224 | tf_op jit(solution)/shard_map/ppermute | solution.py:203
  7.3 13.1 %collective-permute-start.2 = (bf16[128,512]{1,0:T(8,128)(2,1)}, bf16[128,512]{1,0:T(8,128)(2,1)S(1)}, u32[]{:S(2)}, u32[]{:S(2)}) collective-permute-start(bf16[128,512]{1,0:T(8,128)(2,1)} %refs_0_.2), channel_id=1, source_target_pairs={{0,8},{4,12},{8,0},{12,4},{16,24},{20,28},{24,16},{28,20},{1,9},{5... | collective-permute-start | bytes 393224 | tf_op jit(solution)/shard_map/ppermute | solution.py:203
  38.9 12.2 %collective-permute-start.10 = (bf16[128,512]{1,0:T(8,128)(2,1)}, bf16[128,512]{1,0:T(8,128)(2,1)S(1)}, u32[]{:S(2)}, u32[]{:S(2)}) collective-permute-start(bf16[128,512]{1,0:T(8,128)(2,1)} %refs_0_.2), channel_id=1, source_target_pairs={{0,0},{1,8},{2,16},{3,24},{4,4},{5,12},{6,20},{7,28},{8,1},{9,9},{... | collective-permute-start | bytes 393224 | tf_op jit(solution)/shard_map/ppermute | solution.py:214
  59.0 71.5 %collective-permute-start.31 = (bf16[1536,1024]{1,0:T(8,128)(2,1)S(1)}, bf16[1536,1024]{1,0:T(8,128)(2,1)}, u32[]{:S(2)}, u32[]{:S(2)}) collective-permute-start(bf16[1536,1024]{1,0:T(8,128)(2,1)S(1)} %copy-done), channel_id=1, source_target_pairs={{0,2},{1,3},{2,0},{3,1},{4,6},{5,7},{6,4},{7,5},{8,10},{9,11},{10,... | collective-permute-start | bytes 9437192 | tf_op jit(solution)/shard_map/ppermute | solution.py:203
  62.7 14.3 %collective-permute-start.11 = (bf16[128,512]{1,0:T(8,128)(2,1)S(1)}, bf16[128,512]{1,0:T(8,128)(2,1)S(1)}, u32[]{:S(2)}, u32[]{:S(2)}) collective-permute-start(bf16[128,512]{1,0:T(8,128)(2,1)S(1)} %get-tuple-element.51), channel_id=1, source_target_pairs={{0,8},{4,12},{8,0},{12,4},{16,24},{20,28},{24,16},{28,20},{1,9},{5... | collective-permute-start | bytes 393224 | tf_op jit(solution)/shard_map/ppermute | solution.py:203
  63.6 14.9 %collective-permute-start.12 = (bf16[128,512]{1,0:T(8,128)(2,1)S(1)}, bf16[128,512]{1,0:T(8,128)(2,1)S(1)}, u32[]{:S(2)}, u32[]{:S(2)}) collective-permute-start(bf16[128,512]{1,0:T(8,128)(2,1)S(1)} %get-tuple-element.52), channel_id=1, source_target_pairs={{0,12},{4,8},{8,4},{12,0},{16,28},{20,24},{24,20},{28,16},{1,13},{... | collective-permute-start | bytes 393224 | tf_op jit(solution)/shard_map/ppermute | solution.py:203
  64.7 13.8 %collective-permute-start.13 = (bf16[128,512]{1,0:T(8,128)(2,1)S(1)}, bf16[128,512]{1,0:T(8,128)(2,1)S(1)}, u32[]{:S(2)}, u32[]{:S(2)}) collective-permute-start(bf16[128,512]{1,0:T(8,128)(2,1)S(1)} %get-tuple-element.54), channel_id=1, source_target_pairs={{0,4},{4,0},{8,12},{12,8},{16,20},{20,16},{24,28},{28,24},{1,5},{5... | collective-permute-start | bytes 393224 | tf_op jit(solution)/shard_map/ppermute | solution.py:203
  75.1 11.7 %collective-permute-start.15 = (bf16[128,512]{1,0:T(8,128)(2,1)S(1)}, bf16[128,512]{1,0:T(8,128)(2,1)S(1)}, u32[]{:S(2)}, u32[]{:S(2)}) collective-permute-start(bf16[128,512]{1,0:T(8,128)(2,1)S(1)} %add_convert_fusion.6), channel_id=1, source_target_pairs={{0,16},{4,20},{8,24},{12,28},{16,0},{20,4},{24,8},{28,12},{1,17},{... | collective-permute-start | bytes 393224 | tf_op jit(solution)/shard_map/ppermute | solution.py:203
  89.2 12.8 %collective-permute-start.21 = (bf16[128,512]{1,0:T(8,128)(2,1)S(1)}, bf16[128,512]{1,0:T(8,128)(2,1)}, u32[]{:S(2)}, u32[]{:S(2)}) collective-permute-start(bf16[128,512]{1,0:T(8,128)(2,1)S(1)} %add_convert_fusion.4.refs_0_), channel_id=1, source_target_pairs={{0,16},{4,20},{8,24},{12,28},{16,0},{20,4},{24,8},{28,12},{1,17},{... | collective-permute-start | bytes 393224 | tf_op jit(solution)/shard_map/ppermute | solution.py:203
  91.4 12.3 %collective-permute-start.19 = (bf16[128,512]{1,0:T(8,128)(2,1)S(1)}, bf16[128,512]{1,0:T(8,128)(2,1)}, u32[]{:S(2)}, u32[]{:S(2)}) collective-permute-start(bf16[128,512]{1,0:T(8,128)(2,1)S(1)} %add_convert_fusion.4.refs_0_), channel_id=1, source_target_pairs={{0,8},{4,12},{8,0},{12,4},{16,24},{20,28},{24,16},{28,20},{1,9},{5... | collective-permute-start | bytes 393224 | tf_op jit(solution)/shard_map/ppermute | solution.py:203
  91.6 13.2 %collective-permute-start.18 = (bf16[128,512]{1,0:T(8,128)(2,1)S(1)}, bf16[128,512]{1,0:T(8,128)(2,1)}, u32[]{:S(2)}, u32[]{:S(2)}) collective-permute-start(bf16[128,512]{1,0:T(8,128)(2,1)S(1)} %add_convert_fusion.4.refs_0_), channel_id=1, source_target_pairs={{0,4},{4,0},{8,12},{12,8},{16,20},{20,16},{24,28},{28,24},{1,5},{5... | collective-permute-start | bytes 393224 | tf_op jit(solution)/shard_map/ppermute | solution.py:203
  93.9 10.8 %collective-permute-start.24 = (bf16[128,512]{1,0:T(8,128)(2,1)S(1)}, bf16[128,512]{1,0:T(8,128)(2,1)}, u32[]{:S(2)}, u32[]{:S(2)}) collective-permute-start(bf16[128,512]{1,0:T(8,128)(2,1)S(1)} %collective-permute-done.23.refs_6_), channel_id=1, source_target_pairs={{0,4},{4,0},{8,12},{12,8},{16,20},{20,16},{24,28},{28,24},{1,5},{5... | collective-permute-start | bytes 393224 | tf_op jit(solution)/shard_map/ppermute | solution.py:203
  118.5 38.1 %collective-permute-start.30 = (bf16[1536,1024]{1,0:T(8,128)(2,1)S(1)}, bf16[1536,1024]{1,0:T(8,128)(2,1)}, u32[]{:S(2)}, u32[]{:S(2)}) collective-permute-start(bf16[1536,1024]{1,0:T(8,128)(2,1)S(1)} %copy-done), channel_id=1, source_target_pairs={{0,1},{1,0},{2,3},{3,2},{4,5},{5,4},{6,7},{7,6},{8,9},{9,8},{10,11... | collective-permute-start | bytes 9437192 | tf_op jit(solution)/shard_map/ppermute | solution.py:203
  130.5 26.0 %collective-permute-start.32 = (bf16[1536,1024]{1,0:T(8,128)(2,1)}, bf16[1536,1024]{1,0:T(8,128)(2,1)}, u32[]{:S(2)}, u32[]{:S(2)}) collective-permute-start(bf16[1536,1024]{1,0:T(8,128)(2,1)} %collective-permute-done.31.refs_2_), channel_id=1, source_target_pairs={{0,1},{1,0},{2,3},{3,2},{4,5},{5,4},{6,7},{7,6},{8,9},{9,8},{10,11... | collective-permute-start | bytes 9437192 | tf_op jit(solution)/shard_map/ppermute | solution.py:203
  133.7 11.7 %collective-permute-start.28 = (bf16[128,1536]{1,0:T(8,128)(2,1)}, bf16[128,1536]{1,0:T(8,128)(2,1)}, u32[]{:S(2)}, u32[]{:S(2)}) collective-permute-start(bf16[128,1536]{1,0:T(8,128)(2,1)} %fusion.4), channel_id=1, source_target_pairs={{0,2},{1,3},{2,0},{3,1},{4,6},{5,7},{6,4},{7,5},{8,10},{9,11},{10,... | collective-permute-start | bytes 1179656 | tf_op jit(solution)/shard_map/ppermute | solution.py:203
  136.9 15.8 %all-to-all-start = ((bf16[32,4,1024]{2,1,0:T(4,128)(2,1)}), bf16[32,4,1024]{2,1,0:T(4,128)(2,1)}, u32[]{:S(2)}, u32[]{:S(2)}) async-start(bf16[32,4,1024]{2,1,0:T(4,128)(2,1)} %broadcast_in_dim.6), calls=%async_computation | async-start | bytes 524288 | tf_op jit(solution)/shard_map/all_to_all | solution.py:218
  163.4 12.9 %collective-permute-start.36 = (bf16[128,512]{1,0:T(8,128)(2,1)S(1)}, bf16[128,512]{1,0:T(8,128)(2,1)S(1)}, u32[]{:S(2)}, u32[]{:S(2)}) collective-permute-start(bf16[128,512]{1,0:T(8,128)(2,1)S(1)} %get-tuple-element.73), channel_id=1, source_target_pairs={{0,4},{4,0},{8,12},{12,8},{16,20},{20,16},{24,28},{28,24},{1,5},{5... | collective-permute-start | bytes 393224 | tf_op jit(solution)/shard_map/ppermute | solution.py:203
  171.7 33.1 %collective-permute-start.33 = (bf16[128,512]{1,0:T(8,128)(2,1)}, bf16[128,512]{1,0:T(8,128)(2,1)S(1)}, u32[]{:S(2)}, u32[]{:S(2)}) collective-permute-start(bf16[128,512]{1,0:T(8,128)(2,1)} %get-tuple-element.68), channel_id=1, source_target_pairs={{0,8},{4,12},{8,0},{12,4},{16,24},{20,28},{24,16},{28,20},{1,9},{5... | collective-permute-start | bytes 393224 | tf_op jit(solution)/shard_map/ppermute | solution.py:203
  172.4 32.4 %collective-permute-start.34 = (bf16[128,512]{1,0:T(8,128)(2,1)}, bf16[128,512]{1,0:T(8,128)(2,1)S(1)}, u32[]{:S(2)}, u32[]{:S(2)}) collective-permute-start(bf16[128,512]{1,0:T(8,128)(2,1)} %get-tuple-element.69), channel_id=1, source_target_pairs={{0,12},{4,8},{8,4},{12,0},{16,28},{20,24},{24,20},{28,16},{1,13},{... | collective-permute-start | bytes 393224 | tf_op jit(solution)/shard_map/ppermute | solution.py:203
  174.3 30.5 %collective-permute-start.35 = (bf16[128,512]{1,0:T(8,128)(2,1)}, bf16[128,512]{1,0:T(8,128)(2,1)S(1)}, u32[]{:S(2)}, u32[]{:S(2)}) collective-permute-start(bf16[128,512]{1,0:T(8,128)(2,1)} %get-tuple-element.71), channel_id=1, source_target_pairs={{0,4},{4,0},{8,12},{12,8},{16,20},{20,16},{24,28},{28,24},{1,5},{5... | collective-permute-start | bytes 393224 | tf_op jit(solution)/shard_map/ppermute | solution.py:203
  184.7 20.1 %collective-permute-start.38 = (bf16[128,512]{1,0:T(8,128)(2,1)S(1)}, bf16[128,512]{1,0:T(8,128)(2,1)S(1)}, u32[]{:S(2)}, u32[]{:S(2)}) collective-permute-start(bf16[128,512]{1,0:T(8,128)(2,1)S(1)} %add_convert_fusion.3), channel_id=1, source_target_pairs={{0,16},{4,20},{8,24},{12,28},{16,0},{20,4},{24,8},{28,12},{1,17},{... | collective-permute-start | bytes 393224 | tf_op jit(solution)/shard_map/ppermute | solution.py:203
  185.7 19.1 %collective-permute-start.39 = (bf16[128,512]{1,0:T(8,128)(2,1)S(1)}, bf16[128,512]{1,0:T(8,128)(2,1)S(1)}, u32[]{:S(2)}, u32[]{:S(2)}) collective-permute-start(bf16[128,512]{1,0:T(8,128)(2,1)S(1)} %add_convert_fusion.2), channel_id=1, source_target_pairs={{0,24},{4,28},{8,16},{12,20},{16,8},{20,12},{24,0},{28,4},{1,25},{... | collective-permute-start | bytes 393224 | tf_op jit(solution)/shard_map/ppermute | solution.py:203
  (36 other events, 341.1 us)

commit v2 on v1

--- a/solution.py
+++ b/solution.py
@@ -1,3 +1,4 @@
+import functools
 import math
 
 import jax
@@ -205,12 +206,12 @@
 
 def transpose_places(block):
     gx_count, gy_count = lax.axis_size("gx"), lax.axis_size("gy")
-    halves = gx_count // gy_count
     route = []
     for gx_at in range(gx_count):
         for gy_at in range(gy_count):
-            target = (gy_at * halves + gx_at % halves) * gy_count + gx_at // halves
-            route.append((gx_at * gy_count + gy_at, target))
+            gx_to = gy_at // 2 * 4 + gx_at % 4
+            gy_to = gx_at // 4 * 2 + gy_at % 2
+            route.append((gx_at * gy_count + gy_at, gx_to * gy_count + gy_to))
     return lax.ppermute(block, ("gx", "gy"), route)
 
 
@@ -223,6 +224,7 @@
 
 
 PAIRS = tuple((far, near) for far in range(4) for near in range(2))
+SENT_ORDER = (5, 7, 4, 6, 3, 2, 1, 0)
 
 
 def gather_blocks(block):
@@ -243,11 +245,12 @@
     pairs = [wide(held[far, 0]) + wide(across(held[far, 1], 1)) for far in (2, 3)]
     pairs = [pair.astype(jnp.bfloat16) for pair in pairs]
     if tie is not None:
-        *pairs, _ = lax.optimization_barrier((*pairs, tie))
+        *pairs, tie = lax.optimization_barrier((*pairs, tie))
+    pairs[0], diagonal, beside = lax.optimization_barrier((pairs[0], held[1, 1], held[0, 1]))
     summed = [across(pair, 2 * far) for far, pair in zip((2, 3), pairs)]
-    near = wide(across(held[1, 0], 2)) + wide(across(held[1, 1], 3))
-    near = near + wide(held[0, 0]) + wide(across(held[0, 1], 1))
-    return near + wide(summed[0]) + wide(summed[1])
+    near = wide(across(held[1, 0], 2)) + wide(across(diagonal, 3))
+    near = near + wide(held[0, 0]) + wide(across(beside, 1))
+    return near + wide(summed[0]) + wide(summed[1]), tie
 
 
 def rows_dot(left, weight):
@@ -256,14 +259,24 @@
     )
 
 
+def row_factors(squares, features):
+    factors = lax.rsqrt(squares / features + epsilon)
+    rows = factors.shape[1]
+    return jnp.broadcast_to(factors, (rows, rows)).T[:, :1]
+
+
 def attend_kernel(
+    features,
     place_ref,
     lengths_ref,
     requests_ref,
-    group_ref,
+    kept_ref,
+    received_ref,
+    squares_ref,
     cache_ref,
     out_ref,
     appended_ref,
+    group_ref,
     rows_ref,
     window_ref,
     numer_ref,
@@ -289,6 +302,9 @@
         load(step).start()
     whole_copy = pltpu.make_async_copy(cache_ref, appended_ref, copy_sem)
     whole_copy.start()
+    projected = kept_ref[...] + received_ref[...].astype(jnp.float32)
+    projected = projected * row_factors(squares_ref[...], features)
+    group_ref[...] = projected.astype(group_ref.dtype)
     queries = jnp.concatenate(
         [group_ref[:, head * HD : (head + 1) * HD] for head in range(per_group)], axis=0
     )
@@ -371,22 +387,23 @@
     store.wait()
 
 
-def attend_call(places, lengths, requests, group_cols, cache_rows):
-    new_rows = group_cols.shape[0]
+def attend_call(places, lengths, requests, kept, received, squares, cache_rows, features):
+    new_rows = kept.shape[0]
     query_rows = HEADS // KVH * new_rows
     cache_len = cache_rows.shape[0]
     block_len = min(512, cache_len)
     vmem = pl.BlockSpec(memory_space=pltpu.VMEM)
     anywhere = pl.BlockSpec(memory_space=pl.ANY)
     return pl.pallas_call(
-        attend_kernel,
+        functools.partial(attend_kernel, features),
         out_shape=[
             jax.ShapeDtypeStruct((new_rows, HEADS // KVH * HD), jnp.bfloat16),
             jax.ShapeDtypeStruct(cache_rows.shape, cache_rows.dtype),
         ],
-        in_specs=[pl.BlockSpec(memory_space=pltpu.SMEM)] * 3 + [vmem, anywhere],
+        in_specs=[pl.BlockSpec(memory_space=pltpu.SMEM)] * 3 + [vmem] * 3 + [anywhere],
         out_specs=[vmem, anywhere],
         scratch_shapes=[
+            pltpu.VMEM(kept.shape, jnp.bfloat16),
             pltpu.VMEM((cache_len // block_len, block_len, 2 * HD), jnp.bfloat16),
             pltpu.VMEM((new_rows + 16, 2 * HD), jnp.bfloat16),
             pltpu.VMEM((HD, query_rows), jnp.float32),
@@ -396,249 +413,244 @@
             pltpu.SemaphoreType.DMA,
             pltpu.SemaphoreType.DMA,
         ],
-        compiler_params=pltpu.CompilerParams(vmem_limit_bytes=24 * 1024 * 1024),
+        compiler_params=pltpu.CompilerParams(vmem_limit_bytes=12 * 1024 * 1024),
         cost_estimate=pl.CostEstimate(
             flops=4 * query_rows * cache_len * HD,
             bytes_accessed=4 * cache_rows.size,
             transcendentals=query_rows * cache_len,
         ),
-    )(places, lengths, requests, group_cols, cache_rows)
-
-
-def project_near_kernel(place_ref, *refs):
-    piece_refs, gain_ref, weights = refs[:8], refs[8], refs[9:11]
-    normed_ref, out_ref = refs[11:]
-    gy_place, z_place, x_place = (place_ref[at] for at in range(3))
-    rows, width = piece_refs[0].shape
-    squares = jnp.zeros((rows, width), jnp.float32)
-    for piece_ref in piece_refs:
-        values = piece_ref[...].astype(jnp.float32)
-        squares = squares + values * values
-    mean_square = jnp.sum(squares, axis=1, keepdims=True) / (len(piece_refs) * width)
-    factor = lax.rsqrt(mean_square + epsilon)
-    for (far, near), piece_ref in zip(PAIRS, piece_refs):
-        block, half = z_place ^ far, x_place ^ near
-        values = piece_ref[...].astype(jnp.float32) * factor
-        values = values * gain_ref[2 * block + half].astype(jnp.float32)
-        normed_ref[block, half] = values.astype(jnp.bfloat16)
-    total = jnp.zeros(out_ref.shape, jnp.float32)
-    for offset, weight in enumerate(weights):
-        for half in range(2):
-            total = total + jnp.dot(
-                normed_ref[gy_place ^ offset, half],
-                weight[half * width : (half + 1) * width],
-                preferred_element_type=jnp.float32,
-            )
-    out_ref[...] = total
-
-
-def project_far_kernel(place_ref, normed_ref, near_ref, far, far_near, out_ref):
-    width = normed_ref.shape[3]
-    total = near_ref[...]
-    for offset, weight in ((2, far), (3, far_near)):
-        for half in range(2):
-            total = total + jnp.dot(
-                normed_ref[place_ref[0] ^ offset, half],
-                weight[half * width : (half + 1) * width],
-                preferred_element_type=jnp.float32,
-            )
-    out_ref[...] = total.astype(out_ref.dtype)
+    )(places, lengths, requests, kept, received, squares, cache_rows)
 
 
 SMEM = pl.BlockSpec(memory_space=pltpu.SMEM)
 VMEM = pl.BlockSpec(memory_space=pltpu.VMEM)
-ANYWHERE = pl.BlockSpec(memory_space=pl.ANY)
-
-
-def project_near_call(places, pieces, gain, own, near):
-    rows, width = pieces[0].shape
-    depth, columns = own.shape
-    return pl.pallas_call(
-        project_near_kernel,
-        out_shape=[
-            jax.ShapeDtypeStruct((4, 2, rows, width), jnp.bfloat16),
-            jax.ShapeDtypeStruct((rows, columns), jnp.float32),
-        ],
-        in_specs=[SMEM] + [VMEM] * 11,
-        out_specs=[VMEM] * 2,
-        compiler_params=pltpu.CompilerParams(vmem_limit_bytes=24 * 1024 * 1024),
-        cost_estimate=pl.CostEstimate(
-            flops=4 * rows * depth * columns,
-            bytes_accessed=4 * depth * columns,
-            transcendentals=rows,
-        ),
-    )(places, *pieces, gain.reshape(len(pieces), 1, width), own, near)
-
-
-def project_far_call(places, normed, near, far_weights):
-    rows, columns = near.shape
-    depth = far_weights[0].shape[0]
-    return pl.pallas_call(
-        project_far_kernel,
-        out_shape=jax.ShapeDtypeStruct((rows, columns), jnp.bfloat16),
-        in_specs=[SMEM] + [VMEM] * 4,
-        out_specs=VMEM,
-        compiler_params=pltpu.CompilerParams(vmem_limit_bytes=24 * 1024 * 1024),
-        cost_estimate=pl.CostEstimate(
-            flops=4 * rows * depth * columns,
-            bytes_accessed=4 * depth * columns,
-            transcendentals=0,
-        ),
-    )(places, normed, near, *far_weights)
-
-
-def out_kernel(place_ref, attended_ref, weight_ref, *out_refs):
-    z_place, x_place = place_ref[1], place_ref[2]
-    width = out_refs[0].shape[1]
-    for (far, near), out_ref in zip(PAIRS, out_refs):
-        column = pl.multiple_of((x_place ^ near) * width, width)
-        out_ref[...] = jnp.dot(
-            attended_ref[z_place ^ far],
-            weight_ref[:, pl.ds(column, width)],
-            preferred_element_type=jnp.float32,
-        ).astype(out_ref.dtype)
-
-
-def out_call(places, attended, weight):
-    slots, rows, depth = attended.shape
-    columns = weight.shape[1]
-    piece = jax.ShapeDtypeStruct((rows, columns // 2), jnp.bfloat16)
-    return pl.pallas_call(
-        out_kernel,
-        out_shape=[piece] * 8,
-        in_specs=[SMEM, VMEM, VMEM],
-        out_specs=[VMEM] * 8,
-        compiler_params=pltpu.CompilerParams(vmem_limit_bytes=16 * 1024 * 1024),
-        cost_estimate=pl.CostEstimate(
-            flops=2 * slots * rows * depth * columns,
-            bytes_accessed=2 * depth * columns,
-            transcendentals=0,
-        ),
-    )(places, attended, weight)
-
-
-def up_kernel(place_ref, *refs):
-    sources, gain_ref, weight_source = refs[:8], refs[8], refs[9]
-    sent_ref, kept_ref, last_ref, scaled_ref, piece_ref, weight_ref, sems = refs[10:]
+HBM = pl.BlockSpec(memory_space=pltpu.HBM)
+
+
+def in_hbm(values):
+    return [pltpu.with_memory_space_constraint(value, pltpu.HBM) for value in values]
+
+
+def start_copies(sources, targets, sems):
     copies = [
-        pltpu.make_async_copy(source, piece_ref.at[at], sems.at[at])
-        for at, source in enumerate(sources)
+        pltpu.make_async_copy(source, target, sems.at[at])
+        for at, (source, target) in enumerate(zip(sources, targets))
     ]
-    copies.append(pltpu.make_async_copy(weight_source, weight_ref, sems.at[len(sources)]))
     for copy in copies:
         copy.start()
+    return copies
+
+
+def rows_kernel(place_ref, *refs):
+    sources, gain_ref, weights = refs[:8], refs[8], refs[9:11]
+    sent_out, kept_out, last_ref = refs[11:14]
+    sent_ref, kept_ref, scaled_ref, piece_ref, weight_ref, sems, out_sems = refs[14:]
+    copies = start_copies(
+        [*sources, *weights],
+        [piece_ref.at[at] for at in range(8)] + [weight_ref.at[at] for at in range(2)],
+        sems,
+    )
     gy_place, z_place, x_place = (place_ref[at] for at in range(3))
-    core = gy_place % 2
+    core, pair = gy_place % 2, gy_place // 2
     rows, width = piece_ref.shape[1:]
-    columns = weight_ref.shape[1]
+    columns = weight_ref.shape[2]
     ones = jnp.ones((8, width), jnp.float32)
-    for far in range(4):
-        slot = z_place ^ far
-        squares = jnp.zeros((rows, width), jnp.float32)
+    squares = [jnp.zeros((rows, width), jnp.float32) for _ in range(2)]
+    for far in (0, 1, 2, 3):
+        block = (z_place ^ far) % 2
+        slot = ((z_place ^ far) // 2) ^ pair
         for near in range(2):
             half = x_place ^ near
             copies[2 * far + near].wait()
             values = piece_ref[2 * far + near].astype(jnp.float32)
-            squares = squares + values * values
-            gain = gain_ref[:, pl.ds(pl.multiple_of(half * width, width), width)]
-            scaled_ref[slot % 2, half, slot // 2] = (values * gain).astype(jnp.bfloat16)
+            squares[far // 2] = squares[far // 2] + values * values
+            column = pl.multiple_of((2 * block + half) * width, width)
+            gain = gain_ref[:, pl.ds(column, width)]
+            scaled_ref[block ^ core, half, slot] = (values * gain).astype(jnp.bfloat16)
+    for high in range(2):
         sums = lax.dot_general(
             ones,
-            squares,
+            squares[high],
             (((1,), (1,)), ((), ())),
             precision=lax.Precision.HIGHEST,
             preferred_element_type=jnp.float32,
         )
-        last_ref[slot, :, columns:] = sums[:1]
-    copies[-1].wait()
-    step = 512
-    for parity, out_ref in ((1 - core, sent_ref), (core, kept_ref)):
-        for column in range(0, columns, step):
-            total = jnp.zeros((2 * rows, step), jnp.float32)
+        last_ref[(z_place // 2) ^ high ^ pair, :, columns:] = sums[:1]
+    copies[8].wait()
+    copies[9].wait()
+    step = 256
+    for column in range(0, columns, step):
+        total = jnp.zeros((2 * rows, step), jnp.float32)
+        for block in range(2):
             for half in range(2):
                 total = total + jnp.dot(
-                    scaled_ref[parity, half].reshape(2 * rows, width),
-                    weight_ref[half * width : (half + 1) * width, column : column + step],
+                    scaled_ref[block, half].reshape(2 * rows, width),
+                    weight_ref[block, half * width : (half + 1) * width, column : column + step],
                     preferred_element_type=jnp.float32,
                 )
-            for pair in range(2):
-                last_row = total[(pair + 1) * rows - 1 : (pair + 1) * rows]
-                last_ref[2 * pair + parity, :, column : column + step] = last_row
-            out_ref[:, :, column : column + step] = total.reshape(2, rows, step).astype(
-                out_ref.dtype
-            )
-
-
-def up_call(places, pieces, gain, weight):
+        kept_ref[:, column : column + step] = total[:rows]
+        sent_ref[:, column : column + step] = total[rows:].astype(sent_ref.dtype)
+        last_ref[0, :, column : column + step] = total[rows - 1 : rows]
+        last_ref[1, :, column : column + step] = total[2 * rows - 1 :]
+    for copy in start_copies([sent_ref, kept_ref], [sent_out, kept_out], out_sems):
+        copy.wait()
+
+
+def rows_call(places, pieces, gain, own, near):
     rows, width = pieces[0].shape
-    depth, columns = weight.shape
+    depth, columns = own.shape
     return pl.pallas_call(
-        up_kernel,
+        rows_kernel,
         out_shape=[
-            jax.ShapeDtypeStruct((2, rows, columns), jnp.bfloat16),
-            jax.ShapeDtypeStruct((2, rows, columns), jnp.float32),
-            jax.ShapeDtypeStruct((4, 1, columns + rows), jnp.float32),
+            pltpu.HBM((rows, columns), jnp.bfloat16),
+            pltpu.HBM((rows, columns), jnp.float32),
+            jax.ShapeDtypeStruct((2, 1, columns + rows), jnp.float32),
         ],
-        in_specs=[SMEM] + [ANYWHERE] * 8 + [VMEM, ANYWHERE],
-        out_specs=[VMEM] * 3,
+        in_specs=[SMEM] + [HBM] * 8 + [VMEM] + [HBM] * 2,
+        out_specs=[HBM] * 2 + [VMEM],
         scratch_shapes=[
+            pltpu.VMEM((rows, columns), jnp.bfloat16),
+            pltpu.VMEM((rows, columns), jnp.float32),
             pltpu.VMEM((2, 2, 2, rows, width), jnp.bfloat16),
             pltpu.VMEM((8, rows, width), jnp.bfloat16),
-            pltpu.VMEM((depth, columns), jnp.bfloat16),
-            pltpu.SemaphoreType.DMA((9,)),
+            pltpu.VMEM((2, depth, columns), jnp.bfloat16),
+            pltpu.SemaphoreType.DMA((10,)),
+            pltpu.SemaphoreType.DMA((2,)),
         ],
         compiler_params=pltpu.CompilerParams(vmem_limit_bytes=48 * 1024 * 1024),
         cost_estimate=pl.CostEstimate(
             flops=8 * rows * depth * columns,
-            bytes_accessed=2 * depth * columns,
+            bytes_accessed=4 * depth * columns,
             transcendentals=0,
         ),
-    )(places, *pieces, gain.reshape(1, depth), weight)
-
-
-def down_kernel(place_ref, active_ref, *refs):
-    sources, out_refs, tie_ref, (weight_ref, sems) = refs[:4], refs[4:12], refs[12], refs[13:]
+    )(places, *in_hbm(pieces), gain.reshape(1, 2 * depth), *in_hbm((own, near)))
+
+
+def out_kernel(place_ref, attended_ref, other_ref, own, near, *refs):
+    out_refs, (slots_ref, weight_ref, piece_ref, sems, out_sems) = refs[:8], refs[8:]
+    copies = start_copies(
+        [attended_ref, other_ref, own, near],
+        [slots_ref.at[0], slots_ref.at[1], weight_ref.at[0], weight_ref.at[1]],
+        sems,
+    )
     gy_place, z_place, x_place = (place_ref[at] for at in range(3))
-    copies = [
-        pltpu.make_async_copy(source, weight_ref.at[at], sems.at[at])
-        for at, source in enumerate(sources)
-    ]
-    for copy in copies:
-        copy.start()
+    core, pair = gy_place % 2, gy_place // 2
     width = out_refs[0].shape[1]
     for copy in copies:
         copy.wait()
-    for (far, near), out_ref in zip(PAIRS, out_refs):
+    copies = []
+    for at in SENT_ORDER:
+        far, near_bit = PAIRS[at]
+        block = ((z_place ^ far) % 2) ^ core
+        slot = ((z_place ^ far) // 2) ^ pair
+        column = pl.multiple_of((x_place ^ near_bit) * width, width)
+        piece_ref[at] = jnp.dot(
+            slots_ref[slot],
+            weight_ref[block, :, pl.ds(column, width)],
+            preferred_element_type=jnp.float32,
+        ).astype(piece_ref.dtype)
+        copies.append(pltpu.make_async_copy(piece_ref.at[at], out_refs[at], out_sems.at[at]))
+        copies[-1].start()
+    for copy in copies:
+        copy.wait()
+
+
+def out_call(places, attended, other, own, near):
+    rows, depth = attended.shape
+    columns = own.shape[1]
+    piece = pltpu.HBM((rows, columns // 2), jnp.bfloat16)
+    return pl.pallas_call(
+        out_kernel,
+        out_shape=[piece] * 8,
+        in_specs=[SMEM] + [HBM] * 4,
+        out_specs=[HBM] * 8,
+        scratch_shapes=[
+            pltpu.VMEM((2, rows, depth), jnp.bfloat16),
+            pltpu.VMEM((2, depth, columns), jnp.bfloat16),
+            pltpu.VMEM((8, rows, columns // 2), jnp.bfloat16),
+            pltpu.SemaphoreType.DMA((4,)),
+            pltpu.SemaphoreType.DMA((8,)),
+        ],
+        compiler_params=pltpu.CompilerParams(vmem_limit_bytes=48 * 1024 * 1024),
+        cost_estimate=pl.CostEstimate(
+            flops=8 * rows * depth * columns,
+            bytes_accessed=4 * depth * columns,
+            transcendentals=0,
+        ),
+    )(places, *in_hbm((attended, other, own, near)))
+
+
+def down_kernel(features, place_ref, squares_ref, *refs):
+    sources, out_refs, tie_ref = refs[:8], refs[8:16], refs[16]
+    kept_ref, received_ref, active_ref, weight_ref, piece_ref, sems, out_sems = refs[17:]
+    split = sources[4].shape[0]
+    rows, hidden = kept_ref.shape
+    head, tail = pl.ds(0, split), pl.ds(split, hidden - split)
+    copies = start_copies(
+        sources,
+        [
+            kept_ref,
+            received_ref,
+            weight_ref.at[0],
+            weight_ref.at[1],
+            weight_ref.at[2, head],
+            weight_ref.at[3, head],
+            weight_ref.at[2, tail],
+            weight_ref.at[3, tail],
+        ],
+        sems,
+    )
+    gy_place, z_place, x_place = (place_ref[at] for at in range(3))
+    copies[0].wait()
+    copies[1].wait()
+    up_values = kept_ref[...] + received_ref[...].astype(jnp.float32)
+    rectified = jnp.maximum(up_values * row_factors(squares_ref[...], features), 0.0)
+    active_ref[...] = (rectified * rectified).astype(active_ref.dtype)
+    for copy in copies[2:]:
+        copy.wait()
+    width = piece_ref.shape[2]
+    copies = []
+    for at in SENT_ORDER:
+        far, near_bit = PAIRS[at]
         offset = gy_place ^ z_place ^ far
-        column = pl.multiple_of((x_place ^ near) * width, width)
-        out_ref[...] = jnp.dot(
+        column = pl.multiple_of((x_place ^ near_bit) * width, width)
+        piece_ref[at] = jnp.dot(
             active_ref[...],
             weight_ref[offset, :, pl.ds(column, width)],
             preferred_element_type=jnp.float32,
-        ).astype(out_ref.dtype)
+        ).astype(piece_ref.dtype)
+        copies.append(pltpu.make_async_copy(piece_ref.at[at], out_refs[at], out_sems.at[at]))
+        copies[-1].start()
     tie_ref[...] = jnp.zeros_like(tie_ref)
-
-
-def down_call(places, active, weights):
-    rows, hidden = active.shape
+    for copy in copies:
+        copy.wait()
+
+
+def down_call(places, kept, received, squares, weights, features):
+    rows, hidden = kept.shape
     columns = weights[0].shape[1]
-    piece = jax.ShapeDtypeStruct((rows, columns // 2), jnp.bfloat16)
+    piece = pltpu.HBM((rows, columns // 2), jnp.bfloat16)
     *pieces, tie = pl.pallas_call(
-        down_kernel,
+        functools.partial(down_kernel, features),
         out_shape=[piece] * 8 + [jax.ShapeDtypeStruct((8, 128), jnp.float32)],
-        in_specs=[SMEM, VMEM] + [ANYWHERE] * 4,
-        out_specs=[VMEM] * 9,
+        in_specs=[SMEM, VMEM] + [HBM] * 8,
+        out_specs=[HBM] * 8 + [VMEM],
         scratch_shapes=[
+            pltpu.VMEM((rows, hidden), jnp.float32),
+            pltpu.VMEM((rows, hidden), jnp.bfloat16),
+            pltpu.VMEM((rows, hidden), jnp.bfloat16),
             pltpu.VMEM((4, hidden, columns), jnp.bfloat16),
-            pltpu.SemaphoreType.DMA((4,)),
+            pltpu.VMEM((8, rows, columns // 2), jnp.bfloat16),
+            pltpu.SemaphoreType.DMA((8,)),
+            pltpu.SemaphoreType.DMA((8,)),
         ],
-        compiler_params=pltpu.CompilerParams(vmem_limit_bytes=32 * 1024 * 1024),
+        compiler_params=pltpu.CompilerParams(vmem_limit_bytes=48 * 1024 * 1024),
         cost_estimate=pl.CostEstimate(
             flops=8 * rows * hidden * columns,
             bytes_accessed=8 * hidden * columns,
             transcendentals=0,
         ),
-    )(places, active, *weights)
+    )(places, squares, *in_hbm((kept, received, *weights)))
     return pieces, tie
 
 
@@ -654,10 +666,10 @@
         out_ref[...] = jnp.maximum(out_ref[...], logits)
 
 
-def head_call(head_rows, weight, part):
+def head_call(head_rows, weight, part, parts):
     depth, columns = weight.shape
-    step = min(512, columns // 2)
-    count = columns // 2 // step
+    step = min(1024, columns // parts)
+    count = columns // parts // step
     return pl.pallas_call(
         head_kernel,
         grid=(count,),
@@ -667,10 +679,10 @@
             pl.BlockSpec((depth, step), lambda at: (0, part * count + at)),
         ],
         out_specs=pl.BlockSpec((head_rows.shape[0], step), lambda at: (0, 0)),
-        compiler_params=pltpu.CompilerParams(vmem_limit_bytes=24 * 1024 * 1024),
+        compiler_params=pltpu.CompilerParams(vmem_limit_bytes=48 * 1024 * 1024),
         cost_estimate=pl.CostEstimate(
-            flops=head_rows.shape[0] * depth * columns,
-            bytes_accessed=depth * columns,
+            flops=2 * head_rows.shape[0] * depth * columns // parts,
+            bytes_accessed=2 * depth * columns // parts,
             transcendentals=0,
         ),
     )(head_rows, weight)
@@ -694,92 +706,100 @@
     gy_count = lax.axis_size("gy")
     device_count = gx_count * gy_count
     gx_place, gy_place = lax.axis_index("gx"), lax.axis_index("gy")
-    z_place, x_place, pair_place = gx_place // 2, gx_place % 2, gy_place // 2
+    z_place, x_place = gx_place // 2, gx_place % 2
+    pair_place, core_place = gy_place // 2, gy_place % 2
     places = jnp.stack([gy_place, z_place, x_place])
     rows, width = tokens.shape
     features = gx_count * width
     own_features, hidden_units = up_weight.shape
 
-    def pick(blocks, place):
-        return lax.dynamic_index_in_dim(blocks, place, 0, keepdims=False)
-
     def to_all(block):
         pieces = jnp.broadcast_to(block[None], (device_count,) + block.shape)
         return exchange(pieces, ("gx", "gy")).reshape((gx_count, gy_count) + block.shape)
 
-    far_qkv = xor_permute(qkv_weight, "gy", 2)
-    near_qkv = xor_permute(qkv_weight, "gy", 1)
-    normed, near_terms = project_near_call(
-        places, gather_blocks(tokens), attn_gain, qkv_weight, near_qkv
-    )
-    far_qkv, normed, near_terms = lax.optimization_barrier((far_qkv, normed, near_terms))
-    far_weights = (far_qkv, xor_permute(far_qkv, "gy", 1))
-    group_cols = project_far_call(places, normed, near_terms, far_weights)
-    held = transpose_places(tokens)
-
+    def chip_gain(gain):
+        start = pair_place * 2 * own_features
+        return lax.dynamic_slice_in_dim(gain, start, 2 * own_features, 0).astype(jnp.float32)
+
+    def absolute(values, place):
+        swapped = jnp.stack([values[1], values[0]])
+        return jnp.where(place == 0, values, swapped)
+
+    early = hidden_units // 3
+    held, near_qkv, early_rows, late_rows = lax.optimization_barrier(
+        (
+            transpose_places(tokens),
+            xor_permute(qkv_weight, "gy", 1),
+            down_weight[:early],
+            down_weight[early:],
+        )
+    )
+    early_far = xor_permute(early_rows, "gy", 2)
+    blocks = gather_blocks(held)
+    sent, kept, last = rows_call(
+        places, blocks, chip_gain(attn_gain), qkv_weight, near_qkv
+    )
+    sent, early_far, out_source, up_source, down_source = lax.optimization_barrier(
+        (sent, early_far, out_weight, up_weight, down_weight)
+    )
+    near_out, near_up, near_down, early_near = (
+        xor_permute(part, "gy", 1) for part in (out_source, up_source, down_source, early_far)
+    )
+    received = xor_permute(sent, "gy", 2)
+    squares = last[:, :, qkv_weight.shape[1] :]
+    squares = squares[0] + xor_permute(squares[1], "gy", 2)
     attended, appended = attend_call(
-        places, cache_lengths, slot_request, group_cols, kv_cache[0]
+        places, cache_lengths, slot_request, kept, received, squares, kv_cache[0], features
     )
     new_cache = appended[None]
 
-    attended, held = lax.optimization_barrier((attended, held))
-    attention = lax.all_gather(attended, "gy", axis=0)
-    sent_weight, attention = lax.optimization_barrier((down_weight, attention))
-    far_down = xor_permute(sent_weight, "gy", 2)
-    near_down = xor_permute(down_weight, "gy", 1)
-
-    middle = held.astype(jnp.float32) + scatter_blocks(out_call(places, attention, out_weight))
-    middle = middle.astype(jnp.bfloat16)
-
-    gain = lax.dynamic_slice_in_dim(mlp_gain, gy_place * own_features, own_features, 0)
-    blocks = gather_blocks(middle)
-    sent, kept, last_up = up_call(places, blocks, gain.astype(jnp.float32), up_weight)
-    moved, _ = lax.optimization_barrier((middle, blocks[-1]))
-    middle_slot = transpose_places(moved)
-    received = xor_permute(sent, "gy", 1)
-    last_up = last_up[:, 0]
-    last_up = last_up + xor_permute(last_up, "gy", 1)
-    other = pick(kept, 1 - pair_place) + pick(received, 1 - pair_place).astype(jnp.float32)
-    other, last_up, middle_slot = lax.optimization_barrier(
-        (other.astype(jnp.bfloat16), last_up, middle_slot)
-    )
-    far_down, _ = lax.optimization_barrier((far_down, other))
-    far_near_down = xor_permute(far_down, "gy", 1)
-    far_up = xor_permute(other, "gy", 2)
-    last_up = last_up + xor_permute(last_up, "gy", 2)
-    factors = lax.rsqrt(last_up[:, hidden_units:] / features + epsilon)
-
-    last_active = jnp.maximum(last_up[:, :hidden_units] * factors[:, rows - 1 :], 0.0)
-    last_terms = rows_dot((last_active * last_active).astype(jnp.bfloat16), down_weight)
-    last_row = middle[rows - 1 :].astype(jnp.float32)
-    blank = jnp.zeros_like(last_terms)
-    last_terms = last_terms + lax.dynamic_update_slice(
-        blank, last_row, (z_place, x_place * width)
-    )
+    other = xor_permute(attended, "gy", 2)
+    late_rows, other, near_out, near_up, near_down, early_near = lax.optimization_barrier(
+        (late_rows, other, near_out, near_up, near_down, early_near)
+    )
+    late_far = xor_permute(late_rows, "gy", 2)
+    terms, _ = scatter_blocks(out_call(places, attended, other, out_weight, near_out))
+    middle = (held.astype(jnp.float32) + terms).astype(jnp.bfloat16)
+    sent, kept, last = rows_call(
+        places, gather_blocks(middle), chip_gain(mlp_gain), up_weight, near_up
+    )
+    received = xor_permute(sent, "gy", 2)
+    last = last[:, 0]
+    last = last + xor_permute(last[::-1], "gy", 2)
+    squares = last[:, hidden_units:]
+    late_near = xor_permute(late_far, "gy", 1)
+    middle_slot = transpose_places(middle)
+
+    factors = lax.rsqrt(squares[:, rows - 1 :] / features + epsilon)
+    last_active = jnp.maximum(last[:, :hidden_units] * factors, 0.0)
+    last_active = (last_active * last_active).astype(jnp.bfloat16)
+    last_terms = jnp.stack([rows_dot(last_active, part) for part in (down_weight, near_down)])
+    last_terms = absolute(absolute(last_terms, core_place).transpose(1, 0, 2), pair_place)
+    last_row = middle[rows - 1 :].astype(jnp.float32)[None]
+    place = (z_place // 2, z_place % 2, x_place * width)
+    last_terms += lax.dynamic_update_slice(jnp.zeros_like(last_terms), last_row, place)
     last_pieces = to_all(last_terms.astype(jnp.bfloat16))
 
-    up_values = pick(kept, pair_place) + pick(received, pair_place).astype(jnp.float32)
-    up_values = up_values + far_up.astype(jnp.float32)
-    rectified = jnp.maximum(up_values * pick(factors, gy_place)[:, None], 0.0)
-    activation = (rectified * rectified).astype(jnp.bfloat16)
-    down_weights = (down_weight, near_down, far_down, far_near_down)
-    pieces, tie = down_call(places, activation, down_weights)
-    last_pieces, _ = lax.optimization_barrier((last_pieces, tie))
+    weights = (down_weight, near_down, early_far, early_near, late_far, late_near)
+    pieces, tie = down_call(places, kept, received, squares[:1], weights, features)
+    last_pieces, tie, middle_slot = lax.optimization_barrier((last_pieces, tie, middle_slot))
     last_hidden = jnp.sum(last_pieces.astype(jnp.float32), axis=0)
-    last_hidden = last_hidden.transpose(1, 0, 2).reshape(gy_count, features)
+    last_hidden = last_hidden.reshape(2, 2, 2, 2, own_features).transpose(2, 1, 0, 3, 4)
+    last_hidden = last_hidden.reshape(gy_count, features)
     last_hidden = last_hidden.astype(jnp.bfloat16).astype(jnp.float32)
     mean_square = jnp.mean(last_hidden * last_hidden, axis=1)
     last_norms = jnp.sqrt(mean_square)
     head_input = (
         last_hidden * lax.rsqrt(mean_square + epsilon)[:, None] * final_gain.astype(jnp.float32)
     ).astype(jnp.bfloat16)
-    first_max = head_call(head_input, head_weight, 0)
-    second_max = head_call(head_input, head_weight, 1)
+    first_max = head_call(head_input, head_weight, 0, 2)
+    hidden_terms, first_max = scatter_blocks(pieces, first_max)
+    second_max = head_call(head_input, head_weight, 1, 2)
     largest = jnp.max(jnp.maximum(first_max, second_max), axis=1)
-    max_logits = jnp.max(to_all(largest), axis=(0, 1))
-
-    hidden_terms = scatter_blocks(pieces, first_max)
+    hidden_terms = hidden_terms + tie[0, 0]
     hidden_out = (middle_slot.astype(jnp.float32) + hidden_terms).astype(jnp.bfloat16)
+    largest, hidden_out = lax.optimization_barrier((to_all(largest), hidden_out))
+    max_logits = jnp.max(largest, axis=(0, 1))
     return (hidden_out, new_cache, last_norms, max_logits, head_input)
 
 

time: 206 us -> 185 us (0.90)
  waiting for transfers between devices: 77.6 us -> 51.5 us
  starting transfers between devices: 52.3 us -> 73.9 us
  blocking collectives: 17.3 us -> 0 us
  other arithmetic: 10.8 us -> 6.1 us
  local copies, waits for them, and re-layouts: 6.76 us -> 10.8 us
    ppermute x38 -> x41, waiting for transfers between devices: 72 us -> 41.9 us  [xor_permute(): lax.ppermute(values, axis, [(place, place ^ distance) for place in range(...]
    ppermute x38 -> x41, starting transfers between devices: 44.7 us -> 63.3 us  [xor_permute(): lax.ppermute(values, axis, [(place, place ^ distance) for place in range(...]
    all_to_all x1 -> x0, blocking collectives: 9.52 us -> none  [exchange(): return lax.all_to_all(blocks, axes, split_axis=0, concat_axis=0, tiled=True)]
    all_gather x1 -> x0, blocking collectives: 7.81 us -> none  [stationary(): attention = lax.all_gather(attended, 'gy', axis=0)]
    slice x1 -> x5, local copies, waits for them, and re-layouts: 0.18 us -> 6.09 us  [the longest x1 3.14 us: stationary(): down_weight[early:]]
    all_to_all x1 -> x2, waiting for transfers between devices: 5.66 us -> 9.54 us  [exchange(): return lax.all_to_all(blocks, axes, split_axis=0, concat_axis=0, tiled=True)]
    unnamed x39 -> x72, local copies, waits for them, and re-layouts: 4.85 us -> 1.82 us
    all_to_all x1 -> x2, starting transfers between devices: 5.36 us -> 8.18 us  [exchange(): return lax.all_to_all(blocks, axes, split_axis=0, concat_axis=0, tiled=True)]
  transfers between devices with their start and end apart: 41 -> 45, of which waited for: 21 -> 17; matrix products, arithmetic and copies ran while one was open for 6% -> 7% of each run, Pallas kernels for 16% -> 22%
where the time goes in v2:
time: 185 us
  starting transfers between devices  73.9 us (40%)
  waiting for transfers between devices  51.5 us (28%)
  Pallas kernels  40.8 us (22%)
  local copies, waits for them, and re-layouts  10.8 us (6%)
  other arithmetic  6.1 us (3%)
    ppermute x41, starting transfers between devices, xor_permute(): lax.ppermute(values, axis, [(place, place ^ distance) for place in range(...  63.3 us
    ppermute x41, waiting for transfers between devices, xor_permute(): lax.ppermute(values, axis, [(place, place ^ distance) for place in range(...  41.9 us
    pallas_call x2, Pallas kernels, head_call(): pl.pallas_call(head_kernel, grid=(count,), out_shape=jax.ShapeDtypeStruct...  14 us
    pallas_call x2, Pallas kernels, rows_call(): pl.pallas_call(rows_kernel, out_shape=[pltpu.HBM((rows, columns), jnp.bfl...  11.7 us
    all_to_all x2, waiting for transfers between devices, exchange(): return lax.all_to_all(blocks, axes, split_axis=0, concat_axis=0, tiled=True)  9.54 us
    pallas_call x1, Pallas kernels, down_call(): pl.pallas_call(functools.partial(down_kernel, features), out_shape=[piece...  8.24 us
    all_to_all x2, starting transfers between devices, exchange(): return lax.all_to_all(blocks, axes, split_axis=0, concat_axis=0, tiled=True)  8.18 us
    pallas_call x1, Pallas kernels, out_call(): pl.pallas_call(out_kernel, out_shape=[piece] * 8, in_specs=[SMEM] + [HBM]...  3.71 us
  transfers between devices with their start and end apart: 45, of which 17 were waited for; matrix products, arithmetic and copies ran while one was open for 7% of the time, Pallas kernels for 22%

profile of v2, /device:TPU:0, one launch (start us, length us, event | category | flops | bytes accessed | tf_op | source)
XLA Modules:
  0.0 185.5 jit_solution(17189696450116379797)
XLA Ops:
  2.7 3.1 %slice.40 = bf16[1024,1024]{1,0:T(8,128)(2,1)} slice(bf16[1536,1024]{1,0:T(8,128)(2,1)} %refs_2_.1), slice={[512:1536], [0:1024]} | slice | bytes 4194304 | tf_op jit(solution)/shard_map/slice | solution.py:734
  8.3 8.0 %collective-permute-start.9 = (bf16[512,1024]{1,0:T(8,128)(2,1)}, bf16[512,1024]{1,0:T(8,128)(2,1)}, u32[]{:S(2)}, u32[]{:S(2)}) collective-permute-start(bf16[512,1024]{1,0:T(8,128)(2,1)} %slice.39), channel_id=1, source_target_pairs={{0,2},{1,3},{2,0},{3,1},{4,6},{5,7},{6,4},{7,5},{8,10},{9,11},{10,... | collective-permute-start | bytes 3145736 | tf_op jit(solution)/shard_map/ppermute | solution.py:204
  24.7 4.6 %collective-permute-done.5.refs_4_ = bf16[128,512]{1,0:T(8,128)(2,1)} collective-permute-done((bf16[128,512]{1,0:T(8,128)(2,1)S(1)}, bf16[128,512]{1,0:T(8,128)(2,1)}, u32[]{:S(2)}, u32[]{:S(2)}) %collective-permute-start.5) | collective-permute-done | bytes 131104 | tf_op jit(solution)/shard_map/ppermute | solution.py:204
  31.5 3.1 %collective-permute-done.6.refs_5_ = bf16[128,512]{1,0:T(8,128)(2,1)} collective-permute-done((bf16[128,512]{1,0:T(8,128)(2,1)}, bf16[128,512]{1,0:T(8,128)(2,1)}, u32[]{:S(2)}, u32[]{:S(2)}) %collective-permute-start.6) | collective-permute-done | bytes 131104 | tf_op jit(solution)/shard_map/ppermute | solution.py:204
  36.1 4.8 %shard_map.155 = (bf16[128,768]{1,0:T(8,128)(2,1)}, f32[128,768]{1,0:T(8,128)}, f32[2,1,896]{2,1,0:T(1,128)S(1)}) custom-call(s32[3]{0:T(128)S(1)} %pad_add_fusion.place_ref, bf16[128,512]{1,0:T(8,128)(2,1)} %copy-done.16, bf16[128,512]{1,0:T(8,128)(2,1)} %collective-permute-done.2.refs_1_, bf16[128,512]{1,0:T(8,128)(2,1)} %copy-done.25, ...), custom_call_target="tpu_custom_call" | custom-call | flops 805306368 | bytes 3145728 | tf_op jit(solution)/shard_map/pallas_call | solution.py:502
  47.1 4.3 %collective-permute-done.10.received_ref = bf16[128,768]{1,0:T(8,128)(2,1)S(1)} collective-permute-done((bf16[128,768]{1,0:T(8,128)(2,1)}, bf16[128,768]{1,0:T(8,128)(2,1)S(1)}, u32[]{:S(2)}, u32[]{:S(2)}) %collective-permute-start.10) | collective-permute-done | bytes 196640 | tf_op jit(solution)/shard_map/ppermute | solution.py:204
  52.5 3.1 %shard_map.156 = (bf16[128,512]{1,0:T(8,128)(2,1)S(1)}, bf16[4096,256]{1,0:T(8,128)(2,1)}) custom-call(s32[3]{0:T(128)S(1)} %pad_add_fusion.place_ref, s32[4]{0:T(128)S(1)} %copy-done.4, s32[4]{0:T(128)S(1)} %copy-done.5, f32[128,768]{1,0:T(8,128)S(1)} %copy-done.3, bf16[128,768]{1,0:T(8,128)(2,1)S(1)} %collective-permute-done.10.received_ref, ...), custom_call_target="tpu_custom_call" | custom-call | flops 1073741824 | bytes 4194304 | tf_op jit(solution)/shard_map/pallas_call | solution.py:397
  55.6 6.5 %collective-permute-start.12 = (bf16[128,512]{1,0:T(8,128)(2,1)S(1)}, bf16[128,512]{1,0:T(8,128)(2,1)S(1)}, u32[]{:S(2)}, u32[]{:S(2)}) collective-permute-start(bf16[128,512]{1,0:T(8,128)(2,1)S(1)} %get-tuple-element.66.attended_ref), channel_id=1, source_target_pairs={{0,2},{1,3},{2,0},{3,1},{4,6},{5,7},{6,4},{7,5},{8,10},{9,11},{10,... | collective-permute-start | bytes 393224 | tf_op jit(solution)/shard_map/ppermute | solution.py:204
  62.0 3.9 %collective-permute-done.12.other_ref = bf16[128,512]{1,0:T(8,128)(2,1)S(1)} collective-permute-done((bf16[128,512]{1,0:T(8,128)(2,1)S(1)}, bf16[128,512]{1,0:T(8,128)(2,1)S(1)}, u32[]{:S(2)}, u32[]{:S(2)}) %collective-permute-start.12) | collective-permute-done | bytes 131104 | tf_op jit(solution)/shard_map/ppermute | solution.py:204
  68.5 3.7 %shard_map.157 = (bf16[128,512]{1,0:T(8,128)(2,1)}, bf16[128,512]{1,0:T(8,128)(2,1)}, bf16[128,512]{1,0:T(8,128)(2,1)}, bf16[128,512]{1,0:T(8,128)(2,1)}, bf16[1...) custom-call(s32[3]{0:T(128)S(1)} %pad_add_fusion.place_ref, ...), custom_call_target="tpu_custom_call" | custom-call | flops 536870912 | bytes 2097152 | tf_op jit(solution)/shard_map/pallas_call | solution.py:562
  75.1 4.5 %collective-permute-done.18 = bf16[128,512]{1,0:T(8,128)(2,1)S(1)} collective-permute-done((bf16[128,512]{1,0:T(8,128)(2,1)}, bf16[128,512]{1,0:T(8,128)(2,1)S(1)}, u32[]{:S(2)}, u32[]{:S(2)}) %collective-permute-start.18) | collective-permute-done | bytes 131104 | tf_op jit(solution)/shard_map/ppermute | solution.py:204
  90.4 3.7 %collective-permute-done.23 = bf16[128,512]{1,0:T(8,128)(2,1)S(1)} collective-permute-done((bf16[128,512]{1,0:T(8,128)(2,1)S(1)}, bf16[128,512]{1,0:T(8,128)(2,1)S(1)}, u32[]{:S(2)}, u32[]{:S(2)}) %collective-permute-start.23) | collective-permute-done | bytes 131104 | tf_op jit(solution)/shard_map/ppermute | solution.py:204
  95.2 3.9 %collective-permute-start.25 = (bf16[128,512]{1,0:T(8,128)(2,1)S(1)}, bf16[128,512]{1,0:T(8,128)(2,1)S(1)}, u32[]{:S(2)}, u32[]{:S(2)}) collective-permute-start(bf16[128,512]{1,0:T(8,128)(2,1)S(1)} %add_convert_fusion.3.refs_0_), channel_id=1, source_target_pairs={{0,8},{4,12},{8,0},{12,4},{16,24},{20,28},{24,16},{28,20},{1,9},{5... | collective-permute-start | bytes 393224 | tf_op jit(solution)/shard_map/ppermute | solution.py:204
  103.7 4.1 %collective-permute-done.27.refs_4_ = bf16[128,512]{1,0:T(8,128)(2,1)S(1)} collective-permute-done((bf16[128,512]{1,0:T(8,128)(2,1)S(1)}, bf16[128,512]{1,0:T(8,128)(2,1)S(1)}, u32[]{:S(2)}, u32[]{:S(2)}) %collective-permute-start.27) | collective-permute-done | bytes 131104 | tf_op jit(solution)/shard_map/ppermute | solution.py:204
  115.1 7.0 %shard_map.158 = (bf16[128,1536]{1,0:T(8,128)(2,1)}, f32[128,1536]{1,0:T(8,128)}, f32[2,1,1664]{2,1,0:T(1,128)S(1)}) custom-call(s32[3]{0:T(128)S(1)} %pad_add_fusion.place_ref, bf16[128,512]{1,0:T(8,128)(2,1)} %copy-done.14, bf16[128,512]{1,0:T(8,128)(2,1)} %copy-done.21, bf16[128,512]{1,0:T(8,128)(2,1)} %copy-done.18, bf16[128,512]{1,0:T(8,128)(2,1)} %copy-done.22, ...), custom_call_target="tpu_custom_call" | custom-call | flops 1610612736 | bytes 6291456 | tf_op jit(solution)/shard_map/pallas_call | solution.py:502
  128.8 4.8 %all-to-all-start = ((bf16[32,2,2,1024]{3,2,1,0:T(2,128)(2,1)}), bf16[32,2,2,1024]{3,2,1,0:T(2,128)(2,1)S(1)}, u32[]{:S(2)}, u32[]{:S(2)}) async-start(bf16[32,2,2,1024]{3,2,1,0:T(2,128)(2,1)} %broadcast_in_dim.26), calls=%async_computation | async-start | bytes 524288 | tf_op jit(solution)/shard_map/all_to_all | solution.py:219
  134.5 8.2 %shard_map.159 = (bf16[128,512]{1,0:T(8,128)(2,1)}, bf16[128,512]{1,0:T(8,128)(2,1)}, bf16[128,512]{1,0:T(8,128)(2,1)}, bf16[128,512]{1,0:T(8,128)(2,1)}, bf16[1...) custom-call(s32[3]{0:T(128)S(1)} %pad_add_fusion.place_ref, ...), custom_call_target="tpu_custom_call" | custom-call | flops 1610612736 | bytes 12582912 | tf_op jit(solution)/shard_map/pallas_call | solution.py:633
  142.8 3.5 %all-to-all-done = bf16[32,2,2,1024]{3,2,1,0:T(2,128)(2,1)S(1)} async-done(((bf16[32,2,2,1024]{3,2,1,0:T(2,128)(2,1)}), bf16[32,2,2,1024]{3,2,1,0:T(2,128)(2,1)S(1)}, u32[]{:S(2)}, u32[]{:S(2)}) %all-to-all-start) | async-done | bytes 262176 | tf_op jit(solution)/shard_map/all_to_all | solution.py:219
  149.2 7.1 %shard_map.160 = f32[4,1024]{1,0:T(4,128)S(1)} custom-call(bf16[4,4096]{1,0:T(4,128)(2,1)S(1)} %multiply_convert_fusion.rows_ref, bf16[4096,4096]{1,0:T(8,128)(2,1)} %weight_ref.3), custom_call_target="tpu_custom_call" | custom-call | flops 67108864 | bytes 16777216 | tf_op jit(solution)/shard_map/pallas_call | solution.py:673
  156.4 3.0 %collective-permute-start.39 = (bf16[128,512]{1,0:T(8,128)(2,1)S(1)}, bf16[128,512]{1,0:T(8,128)(2,1)S(1)}, u32[]{:S(2)}, u32[]{:S(2)}) collective-permute-start(bf16[128,512]{1,0:T(8,128)(2,1)S(1)} %copy-done.34), channel_id=1, source_target_pairs={{0,12},{4,8},{8,4},{12,0},{16,28},{20,24},{24,20},{28,16},{1,13},{... | collective-permute-start | bytes 393224 | tf_op jit(solution)/shard_map/ppermute | solution.py:204
  159.9 3.6 %collective-permute-start.41 = (bf16[128,512]{1,0:T(8,128)(2,1)S(1)}, bf16[128,512]{1,0:T(8,128)(2,1)S(1)}, u32[]{:S(2)}, u32[]{:S(2)}) collective-permute-start(bf16[128,512]{1,0:T(8,128)(2,1)S(1)} %add_convert_fusion.2), channel_id=1, source_target_pairs={{0,16},{4,20},{8,24},{12,28},{16,0},{20,4},{24,8},{28,12},{1,17},{... | collective-permute-start | bytes 393224 | tf_op jit(solution)/shard_map/ppermute | solution.py:204
  165.0 7.0 %shard_map.161 = f32[4,1024]{1,0:T(4,128)S(1)} custom-call(bf16[4,4096]{1,0:T(4,128)(2,1)S(1)} %multiply_convert_fusion.rows_ref, bf16[4096,4096]{1,0:T(8,128)(2,1)} %weight_ref.3), custom_call_target="tpu_custom_call" | custom-call | flops 67108864 | bytes 16777216 | tf_op jit(solution)/shard_map/pallas_call | solution.py:673
  172.7 3.4 %all-to-all-start.1 = ((f32[32,1,4]{2,1,0:T(1,128)}), f32[32,1,4]{2,1,0:T(1,128)S(1)}, u32[]{:S(2)}, u32[]{:S(2)}) async-start(f32[32,1,4]{2,1,0:T(1,128)} %broadcast_in_dim.27), calls=%async_computation.1 | async-start | bytes 32768 | tf_op jit(solution)/shard_map/all_to_all | solution.py:219
  177.2 6.0 %all-to-all-done.1 = f32[32,1,4]{2,1,0:T(1,128)S(1)} async-done(((f32[32,1,4]{2,1,0:T(1,128)}), f32[32,1,4]{2,1,0:T(1,128)S(1)}, u32[]{:S(2)}, u32[]{:S(2)}) %all-to-all-start.1) | async-done | bytes 544 | tf_op jit(solution)/shard_map/all_to_all | solution.py:219
  (188 shorter events, 69.3 us)
Async XLA Ops:
  8.3 32.6 %collective-permute-start.9 = (bf16[512,1024]{1,0:T(8,128)(2,1)}, bf16[512,1024]{1,0:T(8,128)(2,1)}, u32[]{:S(2)}, u32[]{:S(2)}) collective-permute-start(bf16[512,1024]{1,0:T(8,128)(2,1)} %slice.39), channel_id=1, source_target_pairs={{0,2},{1,3},{2,0},{3,1},{4,6},{5,7},{6,4},{7,5},{8,10},{9,11},{10,... | collective-permute-start | bytes 3145736 | tf_op jit(solution)/shard_map/ppermute | solution.py:204
  16.3 13.0 %collective-permute-start.5 = (bf16[128,512]{1,0:T(8,128)(2,1)S(1)}, bf16[128,512]{1,0:T(8,128)(2,1)}, u32[]{:S(2)}, u32[]{:S(2)}) collective-permute-start(bf16[128,512]{1,0:T(8,128)(2,1)S(1)} %collective-permute-done.refs_0_), channel_id=1, source_target_pairs={{0,16},{4,20},{8,24},{12,28},{16,0},{20,4},{24,8},{28,12},{1,17},{... | collective-permute-start | bytes 393224 | tf_op jit(solution)/shard_map/ppermute | solution.py:204
  18.9 11.9 %collective-permute-start.7 = (bf16[128,512]{1,0:T(8,128)(2,1)S(1)}, bf16[128,512]{1,0:T(8,128)(2,1)}, u32[]{:S(2)}, u32[]{:S(2)}) collective-permute-start(bf16[128,512]{1,0:T(8,128)(2,1)S(1)} %collective-permute-done.refs_0_), channel_id=1, source_target_pairs={{0,24},{4,28},{8,16},{12,20},{16,8},{20,12},{24,0},{28,4},{1,25},{... | collective-permute-start | bytes 393224 | tf_op jit(solution)/shard_map/ppermute | solution.py:204
  20.7 10.8 %collective-permute-start.2 = (bf16[128,512]{1,0:T(8,128)(2,1)S(1)}, bf16[128,512]{1,0:T(8,128)(2,1)}, u32[]{:S(2)}, u32[]{:S(2)}) collective-permute-start(bf16[128,512]{1,0:T(8,128)(2,1)S(1)} %collective-permute-done.refs_0_), channel_id=1, source_target_pairs={{0,4},{4,0},{8,12},{12,8},{16,20},{20,16},{24,28},{28,24},{1,5},{5... | collective-permute-start | bytes 393224 | tf_op jit(solution)/shard_map/ppermute | solution.py:204
  40.9 25.1 %collective-permute-start.14 = (bf16[1024,1536]{1,0:T(8,128)(2,1)}, bf16[1024,1536]{1,0:T(8,128)(2,1)S(1)}, u32[]{:S(2)}, u32[]{:S(2)}) collective-permute-start(bf16[1024,1536]{1,0:T(8,128)(2,1)} %refs_9_.3), channel_id=1, source_target_pairs={{0,1},{1,0},{2,3},{3,2},{4,5},{5,4},{6,7},{7,6},{8,9},{9,8},{10,11... | collective-permute-start | bytes 9437192 | tf_op jit(solution)/shard_map/ppermute | solution.py:204
  41.0 25.0 %collective-permute-start.15 = (bf16[1536,1024]{1,0:T(8,128)(2,1)S(1)}, bf16[1536,1024]{1,0:T(8,128)(2,1)S(1)}, u32[]{:S(2)}, u32[]{:S(2)}) collective-permute-start(bf16[1536,1024]{1,0:T(8,128)(2,1)S(1)} %copy-done.6), channel_id=1, source_target_pairs={{0,1},{1,0},{2,3},{3,2},{4,5},{5,4},{6,7},{7,6},{8,9},{9,8},{10,11... | collective-permute-start | bytes 9437192 | tf_op jit(solution)/shard_map/ppermute | solution.py:204
  41.5 24.5 %collective-permute-start.13 = (bf16[512,1024]{1,0:T(8,128)(2,1)S(1)}, bf16[512,1024]{1,0:T(8,128)(2,1)S(1)}, u32[]{:S(2)}, u32[]{:S(2)}) collective-permute-start(bf16[512,1024]{1,0:T(8,128)(2,1)S(1)} %copy-done.11), channel_id=1, source_target_pairs={{0,1},{1,0},{2,3},{3,2},{4,5},{5,4},{6,7},{7,6},{8,9},{9,8},{10,11... | collective-permute-start | bytes 3145736 | tf_op jit(solution)/shard_map/ppermute | solution.py:204
  41.5 24.4 %collective-permute-start.16 = (bf16[512,1024]{1,0:T(8,128)(2,1)}, bf16[512,1024]{1,0:T(8,128)(2,1)S(1)}, u32[]{:S(2)}, u32[]{:S(2)}) collective-permute-start(bf16[512,1024]{1,0:T(8,128)(2,1)} %collective-permute-done.9.refs_4_), channel_id=1, source_target_pairs={{0,1},{1,0},{2,3},{3,2},{4,5},{5,4},{6,7},{7,6},{8,9},{9,8},{10,11... | collective-permute-start | bytes 3145736 | tf_op jit(solution)/shard_map/ppermute | solution.py:204
  55.6 10.3 %collective-permute-start.12 = (bf16[128,512]{1,0:T(8,128)(2,1)S(1)}, bf16[128,512]{1,0:T(8,128)(2,1)S(1)}, u32[]{:S(2)}, u32[]{:S(2)}) collective-permute-start(bf16[128,512]{1,0:T(8,128)(2,1)S(1)} %get-tuple-element.66.attended_ref), channel_id=1, source_target_pairs={{0,2},{1,3},{2,0},{3,1},{4,6},{5,7},{6,4},{7,5},{8,10},{9,11},{10,... | collective-permute-start | bytes 393224 | tf_op jit(solution)/shard_map/ppermute | solution.py:204
  66.0 58.6 %collective-permute-start.33 = (bf16[1024,1024]{1,0:T(8,128)(2,1)}, bf16[1024,1024]{1,0:T(8,128)(2,1)}, u32[]{:S(2)}, u32[]{:S(2)}) collective-permute-start(bf16[1024,1024]{1,0:T(8,128)(2,1)} %slice.40), channel_id=1, source_target_pairs={{0,2},{1,3},{2,0},{3,1},{4,6},{5,7},{6,4},{7,5},{8,10},{9,11},{10,... | collective-permute-start | bytes 6291464 | tf_op jit(solution)/shard_map/ppermute | solution.py:204
  73.7 9.1 %collective-permute-start.22 = (bf16[128,512]{1,0:T(8,128)(2,1)}, bf16[128,512]{1,0:T(8,128)(2,1)S(1)}, u32[]{:S(2)}, u32[]{:S(2)}) collective-permute-start(bf16[128,512]{1,0:T(8,128)(2,1)} %get-tuple-element.84), channel_id=1, source_target_pairs={{0,4},{4,0},{8,12},{12,8},{16,20},{20,16},{24,28},{28,24},{1,5},{5... | collective-permute-start | bytes 393224 | tf_op jit(solution)/shard_map/ppermute | solution.py:204
  74.3 11.4 %collective-permute-start.17 = (bf16[128,512]{1,0:T(8,128)(2,1)}, bf16[128,512]{1,0:T(8,128)(2,1)S(1)}, u32[]{:S(2)}, u32[]{:S(2)}) collective-permute-start(bf16[128,512]{1,0:T(8,128)(2,1)} %get-tuple-element.74), channel_id=1, source_target_pairs={{0,8},{4,12},{8,0},{12,4},{16,24},{20,28},{24,16},{28,20},{1,9},{5... | collective-permute-start | bytes 393224 | tf_op jit(solution)/shard_map/ppermute | solution.py:204
  99.8 9.6 %collective-permute-start.29 = (bf16[128,512]{1,0:T(8,128)(2,1)S(1)}, bf16[128,512]{1,0:T(8,128)(2,1)S(1)}, u32[]{:S(2)}, u32[]{:S(2)}) collective-permute-start(bf16[128,512]{1,0:T(8,128)(2,1)S(1)} %add_convert_fusion.3.refs_0_), channel_id=1, source_target_pairs={{0,24},{4,28},{8,16},{12,20},{16,8},{20,12},{24,0},{28,4},{1,25},{... | collective-permute-start | bytes 393224 | tf_op jit(solution)/shard_map/ppermute | solution.py:204
  124.4 10.1 %collective-permute-start.32 = (bf16[128,1536]{1,0:T(8,128)(2,1)}, bf16[128,1536]{1,0:T(8,128)(2,1)}, u32[]{:S(2)}, u32[]{:S(2)}) collective-permute-start(bf16[128,1536]{1,0:T(8,128)(2,1)} %get-tuple-element.88), channel_id=1, source_target_pairs={{0,2},{1,3},{2,0},{3,1},{4,6},{5,7},{6,4},{7,5},{8,10},{9,11},{10,... | collective-permute-start | bytes 1179656 | tf_op jit(solution)/shard_map/ppermute | solution.py:204
  124.5 10.0 %collective-permute-start.34 = (bf16[1024,1024]{1,0:T(8,128)(2,1)}, bf16[1024,1024]{1,0:T(8,128)(2,1)}, u32[]{:S(2)}, u32[]{:S(2)}) collective-permute-start(bf16[1024,1024]{1,0:T(8,128)(2,1)} %collective-permute-done.33.refs_6_), channel_id=1, source_target_pairs={{0,1},{1,0},{2,3},{3,2},{4,5},{5,4},{6,7},{7,6},{8,9},{9,8},{10,11... | collective-permute-start | bytes 6291464 | tf_op jit(solution)/shard_map/ppermute | solution.py:204
  128.8 17.5 %all-to-all-start = ((bf16[32,2,2,1024]{3,2,1,0:T(2,128)(2,1)}), bf16[32,2,2,1024]{3,2,1,0:T(2,128)(2,1)S(1)}, u32[]{:S(2)}, u32[]{:S(2)}) async-start(bf16[32,2,2,1024]{3,2,1,0:T(2,128)(2,1)} %broadcast_in_dim.26), calls=%async_computation | async-start | bytes 524288 | tf_op jit(solution)/shard_map/all_to_all | solution.py:219
  133.6 9.1 %collective-permute-start.37 = (bf16[128,512]{1,0:T(8,128)(2,1)S(1)}, bf16[128,512]{1,0:T(8,128)(2,1)S(1)}, u32[]{:S(2)}, u32[]{:S(2)}) collective-permute-start(bf16[128,512]{1,0:T(8,128)(2,1)S(1)} %copy-done.15), channel_id=1, source_target_pairs={{0,0},{1,1},{2,16},{3,17},{4,4},{5,5},{6,20},{7,21},{8,8},{9,9},{1... | collective-permute-start | bytes 393224 | tf_op jit(solution)/shard_map/ppermute | solution.py:215
  147.0 9.2 %collective-permute-start.36 = (bf16[128,512]{1,0:T(8,128)(2,1)}, bf16[128,512]{1,0:T(8,128)(2,1)S(1)}, u32[]{:S(2)}, u32[]{:S(2)}) collective-permute-start(bf16[128,512]{1,0:T(8,128)(2,1)} %get-tuple-element.95), channel_id=1, source_target_pairs={{0,4},{4,0},{8,12},{12,8},{16,20},{20,16},{24,28},{28,24},{1,5},{5... | collective-permute-start | bytes 393224 | tf_op jit(solution)/shard_map/ppermute | solution.py:204
  149.0 34.4 %collective-permute-start.38 = (bf16[128,512]{1,0:T(8,128)(2,1)}, bf16[128,512]{1,0:T(8,128)(2,1)S(1)}, u32[]{:S(2)}, u32[]{:S(2)}) collective-permute-start(bf16[128,512]{1,0:T(8,128)(2,1)} %get-tuple-element.100), channel_id=1, source_target_pairs={{0,8},{4,12},{8,0},{12,4},{16,24},{20,28},{24,16},{28,20},{1,9},{5... | collective-permute-start | bytes 393224 | tf_op jit(solution)/shard_map/ppermute | solution.py:204
  156.4 27.0 %collective-permute-start.39 = (bf16[128,512]{1,0:T(8,128)(2,1)S(1)}, bf16[128,512]{1,0:T(8,128)(2,1)S(1)}, u32[]{:S(2)}, u32[]{:S(2)}) collective-permute-start(bf16[128,512]{1,0:T(8,128)(2,1)S(1)} %copy-done.34), channel_id=1, source_target_pairs={{0,12},{4,8},{8,4},{12,0},{16,28},{20,24},{24,20},{28,16},{1,13},{... | collective-permute-start | bytes 393224 | tf_op jit(solution)/shard_map/ppermute | solution.py:204
  159.4 24.0 %collective-permute-start.40 = (bf16[128,512]{1,0:T(8,128)(2,1)S(1)}, bf16[128,512]{1,0:T(8,128)(2,1)S(1)}, u32[]{:S(2)}, u32[]{:S(2)}) collective-permute-start(bf16[128,512]{1,0:T(8,128)(2,1)S(1)} %copy-done.33), channel_id=1, source_target_pairs={{0,4},{4,0},{8,12},{12,8},{16,20},{20,16},{24,28},{28,24},{1,5},{5... | collective-permute-start | bytes 393224 | tf_op jit(solution)/shard_map/ppermute | solution.py:204
  159.9 23.5 %collective-permute-start.41 = (bf16[128,512]{1,0:T(8,128)(2,1)S(1)}, bf16[128,512]{1,0:T(8,128)(2,1)S(1)}, u32[]{:S(2)}, u32[]{:S(2)}) collective-permute-start(bf16[128,512]{1,0:T(8,128)(2,1)S(1)} %add_convert_fusion.2), channel_id=1, source_target_pairs={{0,16},{4,20},{8,24},{12,28},{16,0},{20,4},{24,8},{28,12},{1,17},{... | collective-permute-start | bytes 393224 | tf_op jit(solution)/shard_map/ppermute | solution.py:204
  163.5 19.9 %collective-permute-start.42 = (bf16[128,512]{1,0:T(8,128)(2,1)S(1)}, bf16[128,512]{1,0:T(8,128)(2,1)S(1)}, u32[]{:S(2)}, u32[]{:S(2)}) collective-permute-start(bf16[128,512]{1,0:T(8,128)(2,1)S(1)} %add_convert_fusion.1), channel_id=1, source_target_pairs={{0,24},{4,28},{8,16},{12,20},{16,8},{20,12},{24,0},{28,4},{1,25},{... | collective-permute-start | bytes 393224 | tf_op jit(solution)/shard_map/ppermute | solution.py:204
  172.7 10.5 %all-to-all-start.1 = ((f32[32,1,4]{2,1,0:T(1,128)}), f32[32,1,4]{2,1,0:T(1,128)S(1)}, u32[]{:S(2)}, u32[]{:S(2)}) async-start(f32[32,1,4]{2,1,0:T(1,128)} %broadcast_in_dim.27), calls=%async_computation.1 | async-start | bytes 32768 | tf_op jit(solution)/shard_map/all_to_all | solution.py:219
  (56 other events, 821.9 us)
